TPU v7x, 32 devices: a whole 2x2x4 slice. The times are simulated.
32 devices in a mesh: dom: 8 (over z, x), grp: 4 (over y, core).
Axes of the slice: x: 2, y: 2, z: 4, core: 2. Of those that a mesh axis runs over, the one named last changes fastest.
Arguments:
- nodes: bfloat16 [32768, 256], P(('dom', 'grp')), may hold values from -6 to 6
- edges: bfloat16 [131072, 256], P(('dom', 'grp')), may hold values from -6 to 6
- senders: int32 [131072], P(('dom', 'grp')), may hold values from 0 to 1279, as said below
- receivers: int32 [131072], P(('dom', 'grp')), may hold values from 0 to 1023, as said below
- edge_count: int32 [32], P(('dom', 'grp')), may hold values from 64 to 512, as said below
- halo_rows: int32 [32, 8, 32], P(('dom', 'grp')), may hold values from 0 to 1023, as said below
- aggregates: int32 [32768], P(('dom', 'grp')), may hold values from 0 to 511, as said below
- coarse_edges: bfloat16 [8, 2048, 256], P('dom'), may hold values from -6 to 6
- coarse_senders: int32 [8, 2048], P('dom'), may hold values from 0 to 511
- coarse_receivers: int32 [8, 2048], P('dom'), may hold values from 0 to 127
- cotangent: bfloat16 [32768, 256], P(('dom', 'grp')), may hold values from -6 to 6
- fine_weights: bfloat16 [1792, 256], replicated, may hold values from -0.21875 to 0.21875
- coarse_weights: bfloat16 [1792, 256], replicated, may hold values from -0.21875 to 0.21875
Outputs:
- fine_out: bfloat16 [32768, 256], P(('dom', 'grp'))
- node_grad: bfloat16 [32768, 256], P(('dom', 'grp'))
- edge_grad: bfloat16 [131072, 256], P(('dom', 'grp'))
- fine_weight_grad: float32 [1792, 256], replicated
- coarse_weight_grad: float32 [1792, 256], replicated
Inputs may be any that keep to these rules, and one draw needn't show every extreme that they name: `senders`: A value at least 1024 names a halo slot from a partition at another dom index with the same grp index. The receivers of edge slots 512 * t to 512 * t + 511 of a partition lie in its node rows 128 * t to 128 * t + 127. `edge_count`: each count is 512 divided by a power of two; some partition has 512 and some 64. `halo_rows`: entry [q, p, t] is a local node row of partition q; the rows of one list are distinct. `aggregates`: every coarse node of a group is the aggregate of exactly 8 fine nodes of that group.
All inputs are finite; a program needn't handle non-finite values.
Results may differ from a plain program's by a relative error of at most 0.035.
Values may be sent and summed in bfloat16 or wider, within the bound.
No kernel may reach another device: no remote copies, remote signals or barrier semaphores. Data moves between devices by JAX's collectives and lax.ppermute only.
A program may use at most 128 MiB of HBM per device.

v0:
```python
import functools

import jax
import jax.numpy as jnp
from jax import lax
from jax.experimental import pallas as pl
from jax.experimental.pallas import tpu as pltpu
from jax.sharding import PartitionSpec as P

F32 = jnp.float32
BF16 = jnp.bfloat16
ROWS = 128
MIB = 1024 * 1024
CHUNK = 32
I16 = jnp.int16


def mm(a, b):
    return lax.dot_general(a, b, (((1,), (0,)), ((), ())), preferred_element_type=F32)


def mm_nt(a, b):
    return lax.dot_general(a, b, (((1,), (1,)), ((), ())), preferred_element_type=F32)


def mm_tn(a, b):
    return lax.dot_general(a, b, (((0,), (0,)), ((), ())), preferred_element_type=F32)


def column(row):
    return jnp.broadcast_to(row, (128, row.shape[1])).T.astype(I16)


def flags(mask):
    return jnp.where(mask, jnp.ones((), BF16), jnp.zeros((), BF16))


def pick_rows(rows, width):
    lane = lax.broadcasted_iota(jnp.int32, (rows[0].shape[1], 128), 1).astype(I16)
    out = []
    for row in rows:
        index = column(row)
        out.append(
            jnp.concatenate([flags(index == lane + I16(128 * k)) for k in range(width // 128)], axis=1)
        )
    return out[0] if len(out) == 1 else jnp.concatenate(out, axis=0)


def pick_columns(rows, height):
    sub = lax.broadcasted_iota(jnp.int32, (height, rows[0].shape[1]), 0).astype(I16)
    out = []
    for row in rows:
        index = jnp.broadcast_to(row, (16, row.shape[1])).astype(I16)
        out.append(flags(sub == jnp.broadcast_to(index[0:1, :], sub.shape)))
    return out[0] if len(out) == 1 else jnp.concatenate(out, axis=1)


def gate(hidden):
    return 0.5 + 0.5 * jnp.tanh(0.5 * hidden)


def normalise(values):
    centre = values - jnp.mean(values, axis=-1, keepdims=True)
    spread = jnp.mean(centre * centre, axis=-1, keepdims=True)
    scale = lax.rsqrt(spread + 1e-05)
    return centre * scale, scale


def normalise_back(grad, unit, scale):
    along = jnp.mean(grad * unit, axis=-1, keepdims=True)
    return scale * (grad - jnp.mean(grad, axis=-1, keepdims=True) - unit * along)


def kernel_call(kernel, micros, limit, **kwargs):
    return pl.pallas_call(
        kernel,
        compiler_params=pltpu.CompilerParams(vmem_limit_bytes=limit * MIB),
        cost_estimate=pl.CostEstimate(
            flops=int(micros * 1.1e9), bytes_accessed=1 << 20, transcendentals=0
        ),
        **kwargs,
    )


def smem():
    return pl.BlockSpec(memory_space=pltpu.SMEM)


def whole(array):
    return pl.BlockSpec(array.shape, lambda t: (0,) * len(array.shape))


def by_tile(rows, columns):
    return pl.BlockSpec((rows, columns), lambda t: (t, 0))


def shape(rows, columns, dtype=BF16):
    return jax.ShapeDtypeStruct((rows, columns), dtype)


def index_rows(ref, start, count):
    return [ref[pl.ds(start + j, 1), :] for j in range(count)]


def live_rows(step, receivers, count, tile, spans):
    lane = lax.broadcasted_iota(jnp.int32, (1, 128), 1)
    parts = tile // 128
    out = []
    for s in range(spans):
        block = step * spans + s
        rows = index_rows(receivers, block * parts, parts)
        out.append(
            [
                jnp.where(lane + 128 * j < count[0], row - block * ROWS, -1)
                for j, row in enumerate(rows)
            ]
        )
    return out


def chunks(total):
    return [slice(r, r + CHUNK) for r in range(0, total, CHUNK)]


def moved(start, here):
    return pl.ds(pl.multiple_of(start + here.start, CHUNK), here.stop - here.start)


def fill_rows(ref, rows, width):
    for j, row in enumerate(rows):
        ref[j * 128 : (j + 1) * 128, :] = pick_rows([row], width)


def my_core():
    return lax.rem(lax.axis_index("grp"), 2)


def split_halves(ref, mine_out, other_out):
    half = mine_out.shape[0]
    core = my_core()
    mine_out[...] = ref[pl.ds(core * half, half), :]
    other_out[...] = ref[pl.ds((1 - core) * half, half), :]


def send_kernel(nodes, halo, near_out, far_out):
    doms, slots = halo.shape
    me = lax.axis_index("dom")
    for first, out in ((0, near_out), (doms // 2, far_out)):
        picks = [
            pick_rows([halo[pl.ds(jnp.bitwise_xor(me, first + r), 1), :]], nodes.shape[0])
            for r in range(doms // 2)
        ]
        out[...] = mm(jnp.concatenate(picks, axis=0), nodes[...]).astype(BF16)


def gather_slots(places, refs, out):
    slots = out.shape[0] // len(places)
    for r, (which, slot) in enumerate(places):
        out[r * slots : (r + 1) * slots, :] = refs[which][slot * slots : (slot + 1) * slots, :]


def group_sums(aggregates, values, mine_out, other_out, sums):
    rows = [aggregates[k : k + 1, :] for k in range(aggregates.shape[0])]
    sums[...] = mm(pick_columns(rows, sums.shape[0]), values).astype(BF16)
    split_halves(sums, mine_out, other_out)


def cotangent_kernel(aggregates, cotangent, mine_out, other_out, sums):
    group_sums(aggregates, cotangent[...], mine_out, other_out, sums)


def fine_local_kernel(
    tile, step_edges, count, edges, senders, receivers, nodes, weights,
    partial_out, send_proj, recv_proj, pick,
):
    width = nodes.shape[1]
    spans = step_edges // tile
    send_proj[...] = mm(nodes[...], weights[width : 2 * width, :]).astype(BF16)
    recv_proj[...] = mm(nodes[...], weights[2 * width : 3 * width, :]).astype(BF16)

    def run(step, carry):
        start = step * step_edges
        send_rows = index_rows(senders, step * spans * (tile // 128), spans * (tile // 128))
        recv_rows = live_rows(step, receivers, count, tile, spans)
        fill_rows(pick, send_rows, nodes.shape[0])
        for s in range(spans):
            own = pl.ds((step * spans + s) * ROWS, ROWS)
            here = slice(s * tile, (s + 1) * tile)
            there = moved(start, here)
            partial_out[there, :] = (
                mm(edges[there, :], weights[:width, :])
                + mm(pick_rows(recv_rows[s], ROWS), recv_proj[own, :])
                + mm(pick[here, :], send_proj[...])
            ).astype(BF16)
        return carry

    lax.fori_loop(0, edges.shape[0] // step_edges, run, 0)


def activate(hidden, active_out, slope_out, here):
    opened = gate(hidden)
    active = hidden * opened
    active_out[here, :] = active.astype(BF16)
    slope_out[here, :] = (opened + active * (1.0 - opened)).astype(BF16)


def fine_halo_kernel(
    tile, places, count, partial, senders, receivers, aggregates, nodes, weights, *refs
):
    pieces = refs[: -(13 + 5)]
    (
    active_out, slope_out, unit_out, scale_out,
    node_active_out, node_slope_out, node_unit_out, node_scale_out, summed_out, refined_out,
    mine_out, other_out, halo,
    halo_proj, pick, wide, wide_next, sums,
    ) = refs[-(13 + 5) :]
    step = pl.program_id(0)
    node_count, width = nodes.shape
    spans = partial.shape[0] // tile

    @pl.when(step == 0)
    def _():
        gather_slots(places, pieces, halo)
        halo_proj[...] = mm(halo[...], weights[width : 2 * width, :]).astype(BF16)

    send_rows = index_rows(senders, step * spans * (tile // 128), spans * (tile // 128))
    recv_rows = live_rows(step, receivers, count, tile, spans)
    mask = lax.axis_index("dom") * (halo.shape[0] // len(places))
    fill_rows(
        pick, [jnp.bitwise_xor(row - node_count, mask) for row in send_rows], halo.shape[0]
    )
    wide[...] = mm(pick[...], halo_proj[...])
    for here in chunks(partial.shape[0]):
        activate(partial[here, :].astype(F32) + wide[here, :], active_out, slope_out, here)
    wide_next[...] = mm(active_out[...], weights[3 * width : 4 * width, :])
    for here in chunks(partial.shape[0]):
        unit, scale = normalise(wide_next[here, :])
        unit_out[here, :] = unit.astype(BF16)
        scale_out[here, :] = scale
    for s in range(spans):
        own = pl.ds((step * spans + s) * ROWS, ROWS)
        summed_out[own, :] = mm(
            pick_columns(recv_rows[s], ROWS), unit_out[s * tile : (s + 1) * tile, :]
        ).astype(BF16)

    @pl.when(step == pl.num_programs(0) - 1)
    def _():
        wide[:node_count, :] = mm(nodes[...], weights[4 * width : 5 * width, :]) + mm(
            summed_out[...], weights[5 * width : 6 * width, :]
        )
        for here in chunks(node_count):
            activate(wide[here, :], node_active_out, node_slope_out, here)
        wide_next[:node_count, :] = mm(node_active_out[...], weights[6 * width :, :])
        for here in chunks(node_count):
            unit, scale = normalise(wide_next[here, :])
            node_unit_out[here, :] = unit.astype(BF16)
            node_scale_out[here, :] = scale
            refined_out[here, :] = (nodes[here, :].astype(F32) + unit).astype(BF16)
        group_sums(aggregates, refined_out[...], mine_out, other_out, sums)


def coarse_kernel(
    groups, chunk,
    table_mine, table_other, cot_mine, cot_other, edges, senders, receivers, weights,
    output_out, grad_out, weight_mine, weight_other,
    table, cot, send_proj, recv_proj, recv_sum, summed, summed_grad,
    node_active, node_slope, node_unit, node_pre, node_hidden_grad,
    active_all, slope_all, unit_all, scale_all, hidden_grad_all, pre_all,
    pick, wide, wide_next, node_scale, own_grad, weight_all,
):
    group_rows, width = table.shape
    half = group_rows // 2
    total = edges.shape[0]
    tile = total // groups
    spans = chunk // tile
    parts = chunk // 128
    steps = total // chunk
    core = my_core()
    mine = pl.ds(core * half, half)
    other = pl.ds((1 - core) * half, half)
    table[mine, :] = table_mine[...]
    table[other, :] = table_other[...]
    cot[mine, :] = cot_mine[...]
    cot[other, :] = cot_other[...]
    send_proj[...] = mm(table[...], weights[width : 2 * width, :]).astype(BF16)
    recv_proj[...] = mm(table[...], weights[2 * width : 3 * width, :]).astype(BF16)

    def recv_at(i, s):
        return index_rows(receivers, i * parts + s * (tile // 128), tile // 128)

    def forward(i, carry):
        start = pl.multiple_of(i * chunk, chunk)
        all_here = pl.ds(start, chunk)
        fill_rows(pick, index_rows(senders, i * parts, parts), group_rows)
        for s in range(spans):
            own = pl.ds((i * spans + s) * ROWS, ROWS)
            here = slice(s * tile, (s + 1) * tile)
            wide[here, :] = (
                mm(edges[pl.ds(start + s * tile, tile), :], weights[:width, :])
                + mm(pick_rows(recv_at(i, s), ROWS), recv_proj[own, :])
                + mm(pick[here, :], send_proj[...])
            )
        for here in chunks(chunk):
            activate(wide[here, :], active_all, slope_all, pl.ds(start + here.start, CHUNK))
        wide_next[...] = mm(active_all[all_here, :], weights[3 * width : 4 * width, :])
        for here in chunks(chunk):
            unit, scale = normalise(wide_next[here, :])
            unit_all[pl.ds(start + here.start, CHUNK), :] = unit.astype(BF16)
            scale_all[pl.ds(start + here.start, CHUNK), :] = scale
        for s in range(spans):
            own = pl.ds((i * spans + s) * ROWS, ROWS)
            summed[own, :] = mm(
                pick_columns(recv_at(i, s), ROWS), unit_all[pl.ds(start + s * tile, tile), :]
            ).astype(BF16)
        return carry

    lax.fori_loop(0, steps, forward, 0)

    nodes_here = slice(0, group_rows)
    wide[nodes_here, :] = mm(table[...], weights[4 * width : 5 * width, :]) + mm(
        summed[...], weights[5 * width : 6 * width, :]
    )
    for here in chunks(group_rows):
        activate(wide[here, :], node_active, node_slope, here)
    wide_next[nodes_here, :] = mm(node_active[...], weights[6 * width :, :])
    for here in chunks(group_rows):
        unit, scale = normalise(wide_next[here, :])
        output_out[here, :] = (table[here, :].astype(F32) + unit).astype(BF16)
        node_pre[here, :] = normalise_back(cot[here, :].astype(F32), unit, scale).astype(BF16)
    wide[nodes_here, :] = mm_nt(node_pre[...], weights[6 * width :, :])
    for here in chunks(group_rows):
        node_hidden_grad[here, :] = (wide[here, :] * node_slope[here, :].astype(F32)).astype(BF16)
    summed_grad[...] = mm_nt(
        node_hidden_grad[...], weights[5 * width : 6 * width, :]
    ).astype(BF16)
    own_grad[...] = mm_nt(node_hidden_grad[...], weights[4 * width : 5 * width, :])

    def backward(i, send_sum):
        start = pl.multiple_of(i * chunk, chunk)
        all_here = pl.ds(start, chunk)
        for s in range(spans):
            own = pl.ds((i * spans + s) * ROWS, ROWS)
            wide[s * tile : (s + 1) * tile, :] = mm(
                pick_rows(recv_at(i, s), ROWS), summed_grad[own, :]
            )
        for here in chunks(chunk):
            there = pl.ds(start + here.start, CHUNK)
            pre_all[there, :] = normalise_back(
                wide[here, :], unit_all[there, :].astype(F32), scale_all[there, :]
            ).astype(BF16)
        wide_next[...] = mm_nt(pre_all[all_here, :], weights[3 * width : 4 * width, :])
        for here in chunks(chunk):
            there = pl.ds(start + here.start, CHUNK)
            hidden_grad_all[there, :] = (
                wide_next[here, :] * slope_all[there, :].astype(F32)
            ).astype(BF16)
        for s in range(spans):
            own = pl.ds((i * spans + s) * ROWS, ROWS)
            recv_sum[own, :] = mm(
                pick_columns(recv_at(i, s), ROWS),
                hidden_grad_all[pl.ds(start + s * tile, tile), :],
            ).astype(BF16)
        return send_sum + mm(
            pick_columns(index_rows(senders, i * parts, parts), group_rows),
            hidden_grad_all[all_here, :],
        )

    send_total = lax.fori_loop(
        0, steps, backward, jnp.zeros((group_rows, width), F32)
    ).astype(BF16)
    recv_total = recv_sum[...]
    grad_out[...] = (
        cot[...].astype(F32)
        + own_grad[...]
        + mm_nt(send_total, weights[width : 2 * width, :])
        + mm_nt(recv_total, weights[2 * width : 3 * width, :])
    ).astype(BF16)
    share = weight_mine.shape[0] * 2
    begin = (core * (groups // 2) + lax.axis_index("grp") // 2) * share
    products = [
        lambda: mm_tn(edges[...], hidden_grad_all[...]),
        lambda: mm_tn(table[...], send_total),
        lambda: mm_tn(table[...], recv_total),
        lambda: mm_tn(active_all[...], pre_all[...]),
        lambda: mm_tn(table[...], node_hidden_grad[...]),
        lambda: mm_tn(summed[...], node_hidden_grad[...]),
        lambda: mm_tn(node_active[...], node_pre[...]),
    ]
    for b, product in enumerate(products):

        @pl.when((b * width < begin + share) & ((b + 1) * width > begin))
        def _():
            weight_all[b * width : (b + 1) * width, :] = product()

    chunk_rows = share // 4
    place = coarse_place()
    for r in range(4):
        first = pl.multiple_of(begin + jnp.bitwise_xor(place, r) * chunk_rows, 8)
        out = (weight_mine, weight_other)[r // 2]
        here = slice((r % 2) * chunk_rows, (r % 2 + 1) * chunk_rows)
        out[here, :] = weight_all[pl.ds(first, chunk_rows), :].astype(BF16)


def coarse_place():
    dom = lax.axis_index("dom")
    return lax.rem(dom, 2) * 2 + lax.rem(dom // 2, 2)


def relative_chunks(ref, place, mine, other):
    rows = ref.shape[0] // 16
    for r in range(16):
        first = pl.multiple_of(jnp.bitwise_xor(place, r) * rows, 16)
        out = (mine, other)[r // 8]
        out[(r % 8) * rows : (r % 8 + 1) * rows, :] = ref[pl.ds(first, rows), :]


def fine_place():
    grp = lax.axis_index("grp")
    return lax.rem(grp, 2) * 8 + lax.rem(grp // 2, 2) * 4 + coarse_place()


def node_back_kernel(
    aggregates, table_grad, cotangent, node_active, node_slope, node_unit, node_scale, summed,
    nodes, weights,
    node_grad_out, summed_grad_out, weight_mine, weight_other,
    pre, hidden_grad, wide, wide_next, weight_out,
):
    node_count, width = nodes.shape
    rows = [aggregates[k : k + 1, :] for k in range(aggregates.shape[0])]
    wide[...] = mm(pick_rows(rows, table_grad.shape[0]), table_grad[...])
    for here in chunks(node_count):
        grad = (cotangent[here, :].astype(F32) + 0.125 * wide[here, :]).astype(BF16)
        grad = grad.astype(F32)
        node_grad_out[here, :] = grad
        pre[here, :] = normalise_back(
            grad, node_unit[here, :].astype(F32), node_scale[here, :]
        ).astype(BF16)
    wide_next[...] = mm_nt(pre[...], weights[6 * width :, :])
    for here in chunks(node_count):
        hidden_grad[here, :] = (
            wide_next[here, :] * node_slope[here, :].astype(F32)
        ).astype(BF16)
    summed_grad_out[...] = mm_nt(
        hidden_grad[...], weights[5 * width : 6 * width, :]
    ).astype(BF16)
    node_grad_out[...] += mm_nt(hidden_grad[...], weights[4 * width : 5 * width, :])
    weight_out[:width, :] = mm_tn(nodes[...], hidden_grad[...]).astype(BF16)
    weight_out[width : 2 * width, :] = mm_tn(summed[...], hidden_grad[...]).astype(BF16)
    weight_out[2 * width :, :] = mm_tn(node_active[...], pre[...]).astype(BF16)
    relative_chunks(weight_out, fine_place(), weight_mine, weight_other)


def edge_back(
    tile, slots, first_step, step_edges, count, edges, active, slope, unit, scale, senders,
    receivers, summed_grad, weights, hidden_grad_out, recv_sum, send_sum, first_grad, second_grad,
    pre, wide, wide_next,
):
    width = weights.shape[1]
    spans = step_edges // tile
    node_count = summed_grad.shape[0]
    mask = lax.axis_index("dom") * slots

    def run(i, carry):
        step = first_step + i
        start = step * step_edges
        begin = i * step_edges
        all_here = moved(start, slice(0, step_edges))
        all_out = moved(begin, slice(0, step_edges))
        send_rows = [
            jnp.where(row < node_count, row, jnp.bitwise_xor(row - node_count, mask) + node_count)
            for row in index_rows(senders, step * spans * (tile // 128), spans * (tile // 128))
        ]
        recv_rows = live_rows(step, receivers, count, tile, spans)
        for s in range(spans):
            own = pl.ds((step * spans + s) * ROWS, ROWS)
            wide[s * tile : (s + 1) * tile, :] = mm(
                pick_rows(recv_rows[s], ROWS), summed_grad[own, :]
            )
        for here in chunks(step_edges):
            there = moved(start, here)
            pre[here, :] = normalise_back(
                wide[here, :], unit[there, :].astype(F32), scale[there, :]
            ).astype(BF16)
        wide_next[...] = mm_nt(pre[...], weights[3 * width : 4 * width, :])
        for here in chunks(step_edges):
            hidden_grad_out[moved(begin, here), :] = (
                wide_next[here, :] * slope[moved(start, here), :].astype(F32)
            ).astype(BF16)
        hidden_grad = hidden_grad_out[all_out, :]
        second_grad[...] += mm_tn(active[all_here, :], pre[...])
        first_grad[...] += mm_tn(edges[all_here, :], hidden_grad)
        send_sum[...] += mm(pick_columns(send_rows, send_sum.shape[0]), hidden_grad)
        for s in range(spans):
            recv_sum[pl.ds((i * spans + s) * ROWS, ROWS), :] = mm(
                pick_columns(recv_rows[s], ROWS),
                hidden_grad_out[moved(begin, slice(s * tile, (s + 1) * tile)), :],
            ).astype(BF16)
        return carry

    lax.fori_loop(0, hidden_grad_out.shape[0] // step_edges, run, 0)


def edge_back_kernel(part, last, tile, slots, step_edges, *refs):
    (
        count, edges, active, slope, unit, scale, senders, receivers, summed_grad, weights,
    ) = refs[:10]
    refs = refs[10:]
    before = ()
    if part:
        before, refs = refs[:3], refs[3:]
    if last:
        nodes, halo, *recv_before = refs[: 2 + part]
        (
            hidden_grad_out, near_out, recv_out, weight_mine, weight_other, halo_near, halo_far,
            recv_sum, send_sum, first_grad, second_grad, pre, wide, wide_next, weight_all,
        ) = refs[2 + part :]
    else:
        (
            hidden_grad_out, recv_sum, send_sum, first_grad, second_grad, pre, wide, wide_next,
        ) = refs
    for i, total in enumerate((send_sum, first_grad, second_grad)):
        total[...] = before[i][...] if part else jnp.zeros_like(total)
    edge_back(
        tile, slots, part, step_edges, count, edges, active, slope, unit, scale, senders,
        receivers, summed_grad, weights, hidden_grad_out, recv_sum, send_sum, first_grad,
        second_grad, pre, wide, wide_next,
    )
    if not last:
        return
    node_count, width = nodes.shape
    send_total = send_sum[...].astype(BF16)
    near, far = send_total[:node_count, :], send_total[node_count:, :]
    for i, rows in enumerate([*recv_before, recv_sum]):
        recv_out[i * rows.shape[0] : (i + 1) * rows.shape[0], :] = rows[...]
    near_out[...] = near
    far_half = far.shape[0] // 2
    send_weights = weights[width : 2 * width, :]
    halo_near[...] = mm_nt(far[:far_half, :], send_weights).astype(BF16)
    halo_far[...] = mm_nt(far[far_half:, :], send_weights).astype(BF16)
    weight_all[:width, :] = first_grad[...].astype(BF16)
    weight_all[width : 2 * width, :] = (mm_tn(nodes[...], near) + mm_tn(halo[...], far)).astype(
        BF16
    )
    weight_all[2 * width : 3 * width, :] = mm_tn(nodes[...], recv_out[...]).astype(BF16)
    weight_all[3 * width : 4 * width, :] = second_grad[...].astype(BF16)
    relative_chunks(weight_all, fine_place(), weight_mine, weight_other)


def edge_out_kernel(weights, *refs):
    step = pl.program_id(0)
    width = weights.shape[1]
    for i, hidden_grad in enumerate(refs[:-1]):

        @pl.when(step == i)
        def _():
            refs[-1][...] = mm_nt(hidden_grad[...], weights[:width, :]).astype(BF16)


def fine_out_kernel(aggregates, table, refined, fine_out):
    rows = [aggregates[k : k + 1, :] for k in range(aggregates.shape[0])]
    lifted = mm(pick_rows(rows, table.shape[0]), table[...])
    fine_out[...] = (refined[...].astype(F32) + lifted).astype(BF16)


def return_kernel(places, halo, node_grad, near, recv_total, weights, *refs):
    doms = len(places)
    pieces, out, values = refs[:-2], refs[-2], refs[-1]
    width = out.shape[1]
    me = lax.axis_index("dom")
    gather_slots(places, pieces, values)
    row = jnp.concatenate(
        [halo[pl.ds(jnp.bitwise_xor(me, r), 1), :] for r in range(doms)], axis=1
    )
    parts = [row[:, 128 * k : 128 * (k + 1)] for k in range(row.shape[1] // 128)]
    out[...] = (
        node_grad[...]
        + mm(pick_columns(parts, out.shape[0]), values[...])
        + mm_nt(near[...], weights[width : 2 * width, :])
        + mm_nt(recv_total[...], weights[2 * width : 3 * width, :])
    ).astype(BF16)


def coarse_final_kernel(chips, scale, mine, other, out):
    step = mine.shape[0] // (4 * chips)
    rows = out.shape[0] // (8 * chips)
    core = my_core()
    chip = lax.axis_index("grp") // 2
    place = coarse_place()
    for which, ref in ((0, mine), (1, other)):
        for c in range(chips):
            member = jnp.bitwise_xor(core, which) * chips + jnp.bitwise_xor(chip, c)
            for r in range(4):
                first = (member * 4 + jnp.bitwise_xor(place, r)) * rows
                here = (c * 4 + r) * step
                out[pl.ds(pl.multiple_of(first, 8), rows), :] = (
                    ref[here : here + rows, :].astype(F32) * scale
                )


def fine_final_kernel(scale, edge_mine, edge_other, node_mine, node_other, out):
    width = out.shape[1]
    place = fine_place()
    rows = 4 * width // 16
    node_rows = 3 * width // 16
    step = node_mine.shape[0] // 8
    for r in range(16):
        at = jnp.bitwise_xor(place, r)
        here = slice((r % 8) * rows, (r % 8 + 1) * rows)
        out[pl.ds(pl.multiple_of(at * rows, 16), rows), :] = (
            (edge_mine, edge_other)[r // 8][here, :].astype(F32) * scale
        )
        end = (r % 8 + 1) * step
        first = pl.multiple_of(4 * width + at * node_rows, 16)
        out[pl.ds(first, node_rows), :] = (
            (node_mine, node_other)[r // 8][end - node_rows : end, :].astype(F32) * scale
        )


def swap_core(value, groups):
    return lax.ppermute(value, "grp", [(i, i ^ 1) for i in range(groups)])


def turn_chip(value, groups, places):
    return lax.ppermute(
        value, "grp", [(i, (i + 2 * places) % groups) for i in range(groups)]
    )


def group_rest(own, scale, groups):
    sent = own.astype(BF16)
    for k in range(1, groups // 2):
        own = own + turn_chip(sent, groups, k).astype(F32)
    return (own * scale).astype(BF16)


def pair_sum(mine, other, groups):
    return mine.astype(F32) + swap_core(other, groups).astype(F32)


def flip(value, axis, bit):
    size = lax.axis_size(axis)
    return lax.ppermute(value, axis, [(i, i ^ (1 << bit)) for i in range(size)])


def add(a, b):
    return (a.astype(F32) + b.astype(F32)).astype(BF16)


def halved(values):
    half = values.shape[0] // 2
    return values[:half], values[half:]


def exchange_slots(near, far, slots):
    doms = lax.axis_size("dom")
    arrays = [near]
    places = [(0, r) for r in range(doms // 2)] + [None] * (doms // 2)
    for bit in reversed(range(doms.bit_length() - 1)):
        moved_slots = [r for r in range(doms) if r >> bit & 1]
        if bit == doms.bit_length() - 2:
            sent = far
        else:
            sent = jnp.concatenate(
                [arrays[w][slot * slots : (slot + 1) * slots] for w, slot in
                 (places[r] for r in moved_slots)],
                axis=0,
            )
        arrays.append(flip(sent, "dom", bit))
        for i, r in enumerate(moved_slots):
            places[r] = (len(arrays) - 1, i)
    return arrays, places


def body(
    nodes,
    edges,
    senders,
    receivers,
    edge_count,
    halo_rows,
    aggregates,
    coarse_edges,
    coarse_senders,
    coarse_receivers,
    cotangent,
    fine_weights,
    coarse_weights,
):
    node_count, width = nodes.shape
    edge_total = edges.shape[0]
    groups = lax.axis_size("grp")
    domains = lax.axis_size("dom")
    devices = groups * domains
    chips = groups // 2
    group_rows = ROWS * groups
    slots = halo_rows.shape[2]
    halo_count = domains * slots
    coarse_total = coarse_senders.shape[1]
    tiles = node_count // ROWS
    tile = edge_total // tiles
    step_edges = 2 * tile
    steps = tiles // 2

    halo_index = halo_rows[0]
    sender_rows = senders.reshape(-1, 128)
    receiver_rows = receivers.reshape(-1, 128)
    aggregate_rows = aggregates.reshape(-1, 128)
    half = shape(group_rows // 2, width)

    def call(kernel, name, micros, outs, ins, scratch=(), limit=20, specs=None, grid=None):
        outs = tuple(outs)
        in_specs, out_specs = specs or (
            [
                smem() if len(leaf.shape) == 1 else pl.BlockSpec(memory_space=pltpu.VMEM)
                for leaf in ins
            ],
            [pl.BlockSpec(memory_space=pltpu.VMEM) for leaf in outs],
        )
        result = kernel_call(
            kernel,
            micros,
            limit,
            out_shape=outs,
            in_specs=in_specs,
            out_specs=out_specs,
            scratch_shapes=list(scratch),
            name=name,
            **({} if grid is None else {"grid": (grid,)}),
        )(*ins)
        return result[0] if len(outs) == 1 else result

    def streamed(kernel, name, micros, outs, ins, scratch=(), limit=20):
        specs = ([whole(leaf) for leaf in ins], [whole(leaf) for leaf in outs])
        return call(kernel, name, micros, outs, ins, scratch, limit, specs, 1)

    def room(rows, columns=width, dtype=BF16):
        return pltpu.VMEM((rows, columns), dtype)

    send_near, send_far = streamed(
        send_kernel, "send_rows", 2,
        [shape(halo_count // 2, width), shape(halo_count // 2, width)], [nodes, halo_index],
    )
    send_far, later_cotangent = lax.optimization_barrier((send_far, cotangent))
    incoming, places = exchange_slots(send_near, send_far, slots)
    cot_mine, cot_other = call(
        cotangent_kernel, "cotangent_sums", 1, [half, half], [aggregate_rows, later_cotangent],
        scratch=[room(group_rows)],
    )
    cot_pair = pair_sum(cot_mine, cot_other, groups)

    partial = call(
        functools.partial(fine_local_kernel, tile, step_edges), "fine_local", 5,
        [shape(edge_total, width)],
        [edge_count, edges, sender_rows, receiver_rows, nodes, fine_weights],
        scratch=[room(node_count), room(node_count), room(step_edges, node_count)],
    )
    partial, cot_pair = lax.optimization_barrier((partial, cot_pair))
    cot_own = group_rest(cot_pair, 1.0, groups)
    per_edge = shape(edge_total, width)
    per_node = shape(node_count, width)
    halo_outs = [
        per_edge, per_edge, per_edge, shape(edge_total, 1, F32), per_node, per_node, per_node,
        shape(node_count, 1, F32), per_node, per_node, half, half, shape(halo_count, width),
    ]
    halo_ins = [
        edge_count, partial, sender_rows, receiver_rows, aggregate_rows, nodes, fine_weights,
        *incoming,
    ]
    (
        active, slope, unit, scale, node_active, node_slope, node_unit, node_scale, summed,
        refined, part_mine, part_other, halo_nodes,
    ) = call(
        functools.partial(fine_halo_kernel, tile, places), "fine_halo", 7, halo_outs, halo_ins,
        scratch=[
            room(halo_count),
            room(step_edges, halo_count),
            room(step_edges, width, F32),
            room(step_edges, width, F32),
            room(group_rows),
        ],
        limit=24,
        specs=(
            [smem(), by_tile(step_edges, width)] + [whole(leaf) for leaf in halo_ins[2:]],
            [by_tile(step_edges, leaf.shape[1]) for leaf in halo_outs[:4]]
            + [whole(leaf) for leaf in halo_outs[4:]],
        ),
        grid=steps,
    )
    part_mine, part_other, cot_own = lax.optimization_barrier((part_mine, part_other, cot_own))
    table_own = group_rest(pair_sum(part_mine, part_other, groups), 0.125, groups)
    tables = [table_own, swap_core(table_own, groups)]
    cots = [cot_own, swap_core(cot_own, groups)]

    coarse_chunk = 2 * coarse_total // groups
    share = 7 * width // groups
    coarse_table, table_grad, coarse_mine, coarse_other = call(
        functools.partial(coarse_kernel, groups, coarse_chunk), "coarse_both_ways", 8,
        [shape(group_rows, width), shape(group_rows, width)] + [shape(share // 2, width)] * 2,
        [
            *tables, *cots, coarse_edges[0], coarse_senders.reshape(-1, 128),
            coarse_receivers.reshape(-1, 128), coarse_weights,
        ],
        scratch=[room(group_rows)] * 12
        + [room(coarse_total)] * 3
        + [room(coarse_total, 1, F32)]
        + [room(coarse_total)] * 2
        + [room(coarse_chunk, group_rows)]
        + [room(max(coarse_chunk, group_rows), width, F32)] * 2
        + [room(group_rows, 1, F32), room(group_rows, width, F32), room(7 * width, width, F32)],
        limit=28,
    )
    half_nodes = shape(3 * width // 2, width)
    node_partial, summed_grad, node_mine, node_other = call(
        node_back_kernel, "node_back", 5,
        [shape(node_count, width, F32), per_node, half_nodes, half_nodes],
        [
            aggregate_rows, table_grad, cotangent, node_active, node_slope, node_unit, node_scale,
            summed, nodes, fine_weights,
        ],
        scratch=[room(node_count)] * 2 + [room(node_count, width, F32)] * 2 + [room(3 * width)],
    )
    fine_out = streamed(
        fine_out_kernel, "fine_out", 2, [per_node], [aggregate_rows, coarse_table, refined]
    )
    more_grp = range(2, groups.bit_length() - 1)
    more_dom = range(2, domains.bit_length() - 1)

    def early_sum():
        mine, other = node_mine, node_other
        for bit in (0, 1):
            received = yield flip(other, "grp", bit)
            mine, other = halved(add(mine, received))
        own = jnp.concatenate([mine, other], axis=0)
        for bit in more_grp:
            own = add(own, (yield flip(own, "grp", bit)))
        n = own.shape[0] // 4
        c = share // 4
        mine, other = (
            jnp.concatenate(
                [
                    coarse[:c], own[2 * k * n : (2 * k + 1) * n],
                    coarse[c:], own[(2 * k + 1) * n : (2 * k + 2) * n],
                ],
                axis=0,
            )
            for k, coarse in enumerate((coarse_mine, coarse_other))
        )
        received = yield flip(other, "dom", 0)
        mine, other = halved(add(mine, received))
        own = add(mine, (yield flip(other, "dom", 1)))
        for bit in more_dom:
            own = add(own, (yield flip(own, "dom", bit)))
        for bit in (1, 0):
            own = jnp.concatenate([own, (yield flip(own, "dom", bit))], axis=0)
        for bit in range(1, groups.bit_length() - 1):
            own = jnp.concatenate([own, (yield flip(own, "grp", bit))], axis=0)
        return own

    early = early_sum()
    moving = next(early)
    moving, summed_grad, fine_out = lax.optimization_barrier((moving, summed_grad, fine_out))

    sources = node_count + halo_count
    square = shape(width, width, F32)
    edge_ins = [
        edge_count, edges, active, slope, unit, scale, sender_rows, receiver_rows, summed_grad,
        fine_weights,
    ]
    edge_room = [room(step_edges), room(step_edges, width, F32), room(step_edges, width, F32)]
    step_shape = shape(step_edges, width)
    recv_shape = shape(node_count // steps, width)
    half_weights = shape(2 * width, width)
    hidden_grads, recv_sums, sums = [], [], []
    for part in range(steps):
        moving = early.send(moving)
        last = part == steps - 1
        kernel = functools.partial(edge_back_kernel, part, last, tile, slots, step_edges)
        if last:
            (
                hidden_grad, near, recv_total, weight_mine, weight_other, halo_near, halo_far
            ) = call(
                kernel, "edge_back_%d" % part, 3,
                [step_shape, per_node, per_node, half_weights, half_weights]
                + [shape(halo_count // 2, width)] * 2,
                edge_ins + sums + [nodes, halo_nodes] + recv_sums,
                scratch=[
                    room(node_count // steps),
                    room(sources, width, F32),
                    room(width, width, F32),
                    room(width, width, F32),
                ]
                + edge_room
                + [room(4 * width)],
            )
            moving, weight_mine, weight_other = lax.optimization_barrier(
                (moving, weight_mine, weight_other)
            )
        else:
            hidden_grad, recv_sum, *sums = call(
                kernel, "edge_back_%d" % part, 2,
                [step_shape, recv_shape, shape(sources, width, F32), square, square],
                edge_ins + sums,
                scratch=edge_room,
            )
            recv_sums.append(recv_sum)
            moving, *sums = lax.optimization_barrier((moving, *sums))
        hidden_grads.append(hidden_grad)

    mine, other = halved(add(weight_mine, flip(weight_other, "grp", 0)))
    other, halo_near, halo_far, *hidden_grads = lax.optimization_barrier(
        (other, halo_near, halo_far, *hidden_grads)
    )
    edge_grad = call(
        edge_out_kernel, "edge_out", 3, [per_edge], [fine_weights, *hidden_grads],
        specs=(
            [whole(fine_weights)] + [whole(leaf) for leaf in hidden_grads],
            [by_tile(step_edges, width)],
        ),
        grid=steps,
    )
    returned, places_back = exchange_slots(halo_near, halo_far, slots)
    received = flip(other, "grp", 1)
    received, edge_grad = lax.optimization_barrier((received, edge_grad))
    mine, other = halved(add(mine, received))
    mine, other = halved(add(mine, flip(other, "dom", 0)))
    own = add(mine, flip(other, "dom", 1))
    for axis, bits in (("grp", more_grp), ("dom", more_dom)):
        for bit in bits:
            own = add(own, flip(own, axis, bit))

    while True:
        try:
            moving = early.send(moving)
        except StopIteration as stop:
            early_mine = stop.value
            break
    early_other = flip(early_mine, "grp", 0)
    weight_shape = shape(7 * width, width, F32)
    coarse_total_grad = streamed(
        functools.partial(coarse_final_kernel, chips, (coarse_total * domains) ** (-0.5)),
        "coarse_weights", 2, [weight_shape], [early_mine, early_other],
    )
    node_grad = streamed(
        functools.partial(return_kernel, places_back), "halo_return", 3, [per_node],
        [halo_index, node_partial, near, recv_total, fine_weights, *returned],
        scratch=[room(halo_count)],
    )
    for axis, bit in (("dom", 1), ("dom", 0)):
        own = jnp.concatenate([own, flip(own, axis, bit)], axis=0)
    own, node_grad = lax.optimization_barrier((own, node_grad))
    own = jnp.concatenate([own, flip(own, "grp", 1)], axis=0)
    own, coarse_total_grad = lax.optimization_barrier((own, coarse_total_grad))
    eight = (early_mine.shape[0] // chips) * 2
    fine_total_grad = streamed(
        functools.partial(fine_final_kernel, (edge_total * devices) ** (-0.5)),
        "fine_weights", 2, [weight_shape],
        [own, flip(own, "grp", 0), early_mine[:eight], early_other[:eight]],
    )
    return (fine_out, node_grad, edge_grad, fine_total_grad, coarse_total_grad)


def solution(mesh):
    placed = (
        P(("dom", "grp"), None),
        P(("dom", "grp"), None),
        P(("dom", "grp")),
        P(("dom", "grp")),
        P(("dom", "grp")),
        P(("dom", "grp"), None, None),
        P(("dom", "grp")),
        P("dom", None, None),
        P("dom", None),
        P("dom", None),
        P(("dom", "grp"), None),
        P(),
        P(),
    )
    return jax.shard_map(
        body,
        mesh=mesh,
        in_specs=placed,
        out_specs=(
            P(("dom", "grp"), None),
            P(("dom", "grp"), None),
            P(("dom", "grp"), None),
            P(),
            P(),
        ),
        check_vma=False,
    )
```

profile of v0, /device:TPU:0, one launch (start us, length us, event | category | flops | bytes accessed | tf_op | source)
XLA Modules:
  0.0 116.3 jit_solution(10485834363311063450)
XLA Ops:
  2.8 4.1 %collective-permute-start.1 = (bf16[128,256]{1,0:T(8,128)(2,1)S(1)}, bf16[128,256]{1,0:T(8,128)(2,1)S(1)}, u32[]{:S(2)}, u32[]{:S(2)}) collective-permute-start(bf16[128,256]{1,0:T(8,128)(2,1)S(1)} %get-tuple-element.96), channel_id=1, source_target_pairs={{0,16},{4,20},{8,24},{12,28},{16,0},{20,4},{24,8},{28,12},{1,17},{... | collective-permute-start | bytes 196616 | tf_op jit(solution)/shard_map/ppermute | solution.py:642
  8.5 2.1 %collective-permute-done.1.refs_1_ = bf16[128,256]{1,0:T(8,128)(2,1)S(1)} collective-permute-done((bf16[128,256]{1,0:T(8,128)(2,1)S(1)}, bf16[128,256]{1,0:T(8,128)(2,1)S(1)}, u32[]{:S(2)}, u32[]{:S(2)}) %collective-permute-start.1) | collective-permute-done | bytes 65568 | tf_op jit(solution)/shard_map/ppermute | solution.py:642
  11.2 4.6 %fine_local.1.partial = bf16[4096,256]{1,0:T(8,128)(2,1)S(1)} custom-call(s32[1]{0:T(128)S(6)} %copy.18.count.refs_0_, bf16[4096,256]{1,0:T(8,128)(2,1)S(1)} %copy-done, s32[32,128]{1,0:T(8,128)S(1)} %bitcast.7, s32[32,128]{1,0:T(8,128)S(1)} %bitcast.13, bf16[1024,256]{1,0:T(8,128)(2,1)S(1)} %copy-done.3, bf16[1792,256]{1,0:T(8,128)(2,1)S(1)} %copy-done.1), custom_call_target="tpu_custom_call" | custom-call | flops 5500000256 | bytes 1048576 | tf_op jit(solution)/shard_map/fine_local/pallas_call | solution.py:719
  20.3 6.4 %fine_halo.1 = (bf16[4096,256]{1,0:T(8,128)(2,1)S(1)}, bf16[4096,256]{1,0:T(8,128)(2,1)S(1)}, bf16[4096,256]{1,0:T(8,128)(2,1)S(1)}, f32[4096,1]{1,0:T(8,128)S(1...) custom-call(s32[1]{0:T(128)S(6)} %copy.18.count.refs_0_, ...), custom_call_target="tpu_custom_call" | custom-call | flops 7699999744 | bytes 1048576 | tf_op jit(solution)/shard_map/fine_halo/pallas_call | solution.py:719
  29.8 4.0 %collective-permute-done.6 = bf16[256,256]{1,0:T(8,128)(2,1)S(1)} collective-permute-done((bf16[256,256]{1,0:T(8,128)(2,1)S(1)}, bf16[256,256]{1,0:T(8,128)(2,1)S(1)}, u32[]{:S(2)}, u32[]{:S(2)}) %collective-permute-start.6) | collective-permute-done | bytes 131104 | tf_op jit(solution)/shard_map/ppermute | solution.py:624
  35.3 10.1 %coarse_both_ways.1 = (bf16[512,256]{1,0:T(8,128)(2,1)S(1)}, bf16[512,256]{1,0:T(8,128)(2,1)S(1)}, bf16[224,256]{1,0:T(8,128)(2,1)S(1)}, bf16[224,256]{1,0:T(8,128)(2,1)S(1)}) custom-call(bf16[256,256]{1,0:T(8,128)(2,1)S(1)} %multiply_convert_fusion.table_mine, bf16[256,256]{1,0:T(8,128)(2,1)S(1)} %collective-permute-done.7.table_other, ...), custom_call_target="tpu_custom_call" | custom-call | flops 8800000000 | bytes 1048576 | tf_op jit(solution)/shard_map/coarse_both_ways/pallas_call | solution.py:719
  45.4 2.1 %node_back.1 = (f32[1024,256]{1,0:T(8,128)S(1)}, bf16[1024,256]{1,0:T(8,128)(2,1)S(1)}, bf16[384,256]{1,0:T(8,128)(2,1)S(1)}, bf16[384,256]{1,0:T(8,128)(2,1)S(1)}) custom-call(s32[8,128]{1,0:T(8,128)S(1)} %bitcast.24, bf16[512,256]{1,0:T(8,128)(2,1)S(1)} %get-tuple-element.103.table_grad, bf16[1024,256]{1,0:T(8,128)(2,1)S(1)} %copy-done.8, ...), custom_call_target="tpu_custom_call" | custom-call | flops 5500000256 | bytes 1048576 | tf_op jit(solution)/shard_map/node_back/pallas_call | solution.py:719
  51.0 2.0 %edge_back_0.1 = (bf16[1024,256]{1,0:T(8,128)(2,1)S(1)}, bf16[256,256]{1,0:T(8,128)(2,1)S(1)}, f32[1280,256]{1,0:T(8,128)S(1)}, f32[256,256]{1,0:T(8,128)S(1)}, f32[256,256]{1,0:T(8,128)S(1)}) custom-call(s32[1]{0:T(128)S(6)} %copy.18.count.refs_0_, bf16[4096,256]{1,0:T(8,128)(2,1)S(1)} %copy-done, bf16[4096,256]{1,0:T(8,128)(2,1)S(1)} %get-tuple-element.117.refs_2_, ...), custom_call_target="tpu_custom_call" | custom-call | flops 2200000000 | bytes 1048576 | tf_op jit(solution)/shard_map/edge_back_0/pallas_call | solution.py:719
  56.0 2.0 %edge_back_1.1 = (bf16[1024,256]{1,0:T(8,128)(2,1)S(1)}, bf16[256,256]{1,0:T(8,128)(2,1)S(1)}, f32[1280,256]{1,0:T(8,128)S(1)}, f32[256,256]{1,0:T(8,128)S(1)}, f32[256,256]{1,0:T(8,128)S(1)}) custom-call(s32[1]{0:T(128)S(6)} %copy.18.count.refs_0_, bf16[4096,256]{1,0:T(8,128)(2,1)S(1)} %copy-done, bf16[4096,256]{1,0:T(8,128)(2,1)S(1)} %get-tuple-element.117.refs_2_, ...), custom_call_target="tpu_custom_call" | custom-call | flops 2200000000 | bytes 1048576 | tf_op jit(solution)/shard_map/edge_back_1/pallas_call | solution.py:719
  58.0 1.9 %collective-permute-done.11 = bf16[320,256]{1,0:T(8,128)(2,1)S(1)} collective-permute-done((bf16[320,256]{1,0:T(8,128)(2,1)S(1)}, bf16[320,256]{1,0:T(8,128)(2,1)S(1)}, u32[]{:S(2)}, u32[]{:S(2)}) %collective-permute-start.11) | collective-permute-done | bytes 163872 | tf_op jit(solution)/shard_map/ppermute | solution.py:642
  60.0 2.0 %collective-permute-start.12 = (bf16[160,256]{1,0:T(8,128)(2,1)S(1)}, bf16[160,256]{1,0:T(8,128)(2,1)S(1)}, u32[]{:S(2)}, u32[]{:S(2)}) collective-permute-start(bf16[160,256]{1,0:T(8,128)(2,1)S(1)} %slice.145), channel_id=1, source_target_pairs={{0,8},{4,12},{8,0},{12,4},{16,24},{20,28},{24,16},{28,20},{1,9},{5... | collective-permute-start | bytes 245768 | tf_op jit(solution)/shard_map/ppermute | solution.py:642
  62.0 2.0 %edge_back_2.1 = (bf16[1024,256]{1,0:T(8,128)(2,1)S(1)}, bf16[256,256]{1,0:T(8,128)(2,1)S(1)}, f32[1280,256]{1,0:T(8,128)S(1)}, f32[256,256]{1,0:T(8,128)S(1)}, f32[256,256]{1,0:T(8,128)S(1)}) custom-call(s32[1]{0:T(128)S(6)} %copy.18.count.refs_0_, bf16[4096,256]{1,0:T(8,128)(2,1)S(1)} %copy-done, bf16[4096,256]{1,0:T(8,128)(2,1)S(1)} %get-tuple-element.117.refs_2_, ...), custom_call_target="tpu_custom_call" | custom-call | flops 2200000000 | bytes 1048576 | tf_op jit(solution)/shard_map/edge_back_2/pallas_call | solution.py:719
  64.5 3.9 %collective-permute-start.13 = (bf16[160,256]{1,0:T(8,128)(2,1)S(1)}, bf16[160,256]{1,0:T(8,128)(2,1)S(1)}, u32[]{:S(2)}, u32[]{:S(2)}) collective-permute-start(bf16[160,256]{1,0:T(8,128)(2,1)S(1)} %add_convert_fusion.7), channel_id=1, source_target_pairs={{0,16},{4,20},{8,24},{12,28},{16,0},{20,4},{24,8},{28,12},{1,17},{... | collective-permute-start | bytes 245768 | tf_op jit(solution)/shard_map/ppermute | solution.py:642
  68.5 3.3 %edge_back_3.1 = (bf16[1024,256]{1,0:T(8,128)(2,1)S(1)}, bf16[1024,256]{1,0:T(8,128)(2,1)S(1)}, bf16[1024,256]{1,0:T(8,128)(2,1)S(1)}, bf16[512,256]{1,0:T(8,128...) custom-call(s32[1]{0:T(128)S(6)} %copy.18.count.refs_0_, ...), custom_call_target="tpu_custom_call" | custom-call | flops 3300000000 | bytes 1048576 | tf_op jit(solution)/shard_map/edge_back_3/pallas_call | solution.py:719
  72.0 4.8 %collective-permute-done.25 = bf16[160,256]{1,0:T(8,128)(2,1)S(1)} collective-permute-done((bf16[160,256]{1,0:T(8,128)(2,1)S(1)}, bf16[160,256]{1,0:T(8,128)(2,1)S(1)}, u32[]{:S(2)}, u32[]{:S(2)}) %collective-permute-start.25) | collective-permute-done | bytes 81952 | tf_op jit(solution)/shard_map/ppermute | solution.py:642
  76.9 1.9 %collective-permute-start.26 = (bf16[320,256]{1,0:T(8,128)(2,1)S(1)}, bf16[320,256]{1,0:T(8,128)(2,1)S(1)}, u32[]{:S(2)}, u32[]{:S(2)}) collective-permute-start(bf16[320,256]{1,0:T(8,128)(2,1)S(1)} %pad_maximum_fusion.4), channel_id=1, source_target_pairs={{0,4},{4,0},{8,12},{12,8},{16,20},{20,16},{24,28},{28,24},{1,5},{5... | collective-permute-start | bytes 491528 | tf_op jit(solution)/shard_map/ppermute | solution.py:642
  80.7 1.9 %collective-permute-start.21 = (bf16[128,256]{1,0:T(8,128)(2,1)S(1)}, bf16[128,256]{1,0:T(8,128)(2,1)S(1)}, u32[]{:S(2)}, u32[]{:S(2)}) collective-permute-start(bf16[128,256]{1,0:T(8,128)(2,1)S(1)} %get-tuple-element.168), channel_id=1, source_target_pairs={{0,16},{4,20},{8,24},{12,28},{16,0},{20,4},{24,8},{28,12},{1,17},{... | collective-permute-start | bytes 196616 | tf_op jit(solution)/shard_map/ppermute | solution.py:642
  82.6 2.6 %edge_out.1 = bf16[4096,256]{1,0:T(8,128)(2,1)} custom-call(bf16[1792,256]{1,0:T(8,128)(2,1)S(1)} %copy-done.1, bf16[1024,256]{1,0:T(8,128)(2,1)S(1)} %get-tuple-element.159.refs_0_, bf16[1024,256]{1,0:T(8,128)(2,1)S(1)} %get-tuple-element.160.refs_1_, bf16[1024,256]{1,0:T(8,128)(2,1)S(1)} %get-tuple-element.161.refs_2_, ...), custom_call_target="tpu_custom_call" | custom-call | flops 3300000000 | bytes 1048576 | tf_op jit(solution)/shard_map/edge_out/pallas_call | solution.py:719
  86.5 3.1 %collective-permute-done.16 = bf16[128,256]{1,0:T(8,128)(2,1)S(1)} collective-permute-done((bf16[128,256]{1,0:T(8,128)(2,1)S(1)}, bf16[128,256]{1,0:T(8,128)(2,1)S(1)}, u32[]{:S(2)}, u32[]{:S(2)}) %collective-permute-start.16) | collective-permute-done | bytes 65568 | tf_op jit(solution)/shard_map/ppermute | solution.py:642
  91.7 1.9 %collective-permute-done.17 = bf16[64,256]{1,0:T(8,128)(2,1)S(1)} collective-permute-done((bf16[64,256]{1,0:T(8,128)(2,1)S(1)}, bf16[64,256]{1,0:T(8,128)(2,1)S(1)}, u32[]{:S(2)}, u32[]{:S(2)}) %collective-permute-start.17) | collective-permute-done | bytes 32800 | tf_op jit(solution)/shard_map/ppermute | solution.py:642
  94.8 3.8 %collective-permute-done.18 = bf16[64,256]{1,0:T(8,128)(2,1)S(1)} collective-permute-done((bf16[64,256]{1,0:T(8,128)(2,1)S(1)}, bf16[64,256]{1,0:T(8,128)(2,1)S(1)}, u32[]{:S(2)}, u32[]{:S(2)}) %collective-permute-start.18) | collective-permute-done | bytes 32800 | tf_op jit(solution)/shard_map/ppermute | solution.py:642
  99.4 3.1 %collective-permute-done.19 = bf16[64,256]{1,0:T(8,128)(2,1)S(1)} collective-permute-done((bf16[64,256]{1,0:T(8,128)(2,1)S(1)}, bf16[64,256]{1,0:T(8,128)(2,1)S(1)}, u32[]{:S(2)}, u32[]{:S(2)}) %collective-permute-start.19) | collective-permute-done | bytes 32800 | tf_op jit(solution)/shard_map/ppermute | solution.py:642
  104.7 2.1 %collective-permute-done.20 = bf16[128,256]{1,0:T(8,128)(2,1)S(1)} collective-permute-done((bf16[128,256]{1,0:T(8,128)(2,1)S(1)}, bf16[128,256]{1,0:T(8,128)(2,1)S(1)}, u32[]{:S(2)}, u32[]{:S(2)}) %collective-permute-start.20) | collective-permute-done | bytes 65568 | tf_op jit(solution)/shard_map/ppermute | solution.py:642
  107.5 4.4 %collective-permute-done.24 = bf16[256,256]{1,0:T(8,128)(2,1)S(1)} collective-permute-done((bf16[256,256]{1,0:T(8,128)(2,1)S(1)}, bf16[256,256]{1,0:T(8,128)(2,1)S(1)}, u32[]{:S(2)}, u32[]{:S(2)}) %collective-permute-start.24) | collective-permute-done | bytes 131104 | tf_op jit(solution)/shard_map/ppermute | solution.py:642
  (123 shorter events, 33.7 us)
Async XLA Ops:
  2.8 7.8 %collective-permute-start.1 = (bf16[128,256]{1,0:T(8,128)(2,1)S(1)}, bf16[128,256]{1,0:T(8,128)(2,1)S(1)}, u32[]{:S(2)}, u32[]{:S(2)}) collective-permute-start(bf16[128,256]{1,0:T(8,128)(2,1)S(1)} %get-tuple-element.96), channel_id=1, source_target_pairs={{0,16},{4,20},{8,24},{12,28},{16,0},{20,4},{24,8},{28,12},{1,17},{... | collective-permute-start | bytes 196616 | tf_op jit(solution)/shard_map/ppermute | solution.py:642
  7.5 10.0 %collective-permute-start = (bf16[256,256]{1,0:T(8,128)(2,1)S(1)}, bf16[256,256]{1,0:T(8,128)(2,1)S(1)}, u32[]{:S(2)}, u32[]{:S(2)}) collective-permute-start(bf16[256,256]{1,0:T(8,128)(2,1)S(1)} %get-tuple-element.93), channel_id=1, source_target_pairs={{0,1},{1,0},{2,3},{3,2},{4,5},{5,4},{6,7},{7,6},{8,9},{9,8},{10,11... | collective-permute-start | bytes 393224 | tf_op jit(solution)/shard_map/ppermute | solution.py:620
  10.6 5.3 %collective-permute-start.2 = (bf16[128,256]{1,0:T(8,128)(2,1)S(1)}, bf16[128,256]{1,0:T(8,128)(2,1)S(1)}, u32[]{:S(2)}, u32[]{:S(2)}) collective-permute-start(bf16[128,256]{1,0:T(8,128)(2,1)S(1)} %pad_maximum_fusion.6), channel_id=1, source_target_pairs={{0,8},{4,12},{8,0},{12,4},{16,24},{20,28},{24,16},{28,20},{1,9},{5... | collective-permute-start | bytes 196616 | tf_op jit(solution)/shard_map/ppermute | solution.py:642
  15.9 4.3 %collective-permute-start.3 = (bf16[128,256]{1,0:T(8,128)(2,1)S(1)}, bf16[128,256]{1,0:T(8,128)(2,1)S(1)}, u32[]{:S(2)}, u32[]{:S(2)}) collective-permute-start(bf16[128,256]{1,0:T(8,128)(2,1)S(1)} %pad_maximum_fusion.7), channel_id=1, source_target_pairs={{0,4},{4,0},{8,12},{12,8},{16,20},{20,16},{24,28},{28,24},{1,5},{5... | collective-permute-start | bytes 196616 | tf_op jit(solution)/shard_map/ppermute | solution.py:642
  17.5 9.2 %collective-permute-start.4 = (bf16[256,256]{1,0:T(8,128)(2,1)S(1)}, bf16[256,256]{1,0:T(8,128)(2,1)S(1)}, u32[]{:S(2)}, u32[]{:S(2)}) collective-permute-start(bf16[256,256]{1,0:T(8,128)(2,1)S(1)} %convert_element_type.122), channel_id=1, source_target_pairs={{0,2},{1,3},{2,0},{3,1},{4,6},{5,7},{6,4},{7,5},{8,10},{9,11},{10,... | collective-permute-start | bytes 393224 | tf_op jit(solution)/shard_map/ppermute | solution.py:624
  28.2 5.6 %collective-permute-start.6 = (bf16[256,256]{1,0:T(8,128)(2,1)S(1)}, bf16[256,256]{1,0:T(8,128)(2,1)S(1)}, u32[]{:S(2)}, u32[]{:S(2)}) collective-permute-start(bf16[256,256]{1,0:T(8,128)(2,1)S(1)} %fusion), channel_id=1, source_target_pairs={{0,2},{1,3},{2,0},{3,1},{4,6},{5,7},{6,4},{7,5},{8,10},{9,11},{10,... | collective-permute-start | bytes 393224 | tf_op jit(solution)/shard_map/ppermute | solution.py:624
  29.8 4.2 %collective-permute-start.8 = (bf16[256,256]{1,0:T(8,128)(2,1)S(1)}, bf16[256,256]{1,0:T(8,128)(2,1)S(1)}, u32[]{:S(2)}, u32[]{:S(2)}) collective-permute-start(bf16[256,256]{1,0:T(8,128)(2,1)S(1)} %add_convert_fusion.4.cot_mine), channel_id=1, source_target_pairs={{0,1},{1,0},{2,3},{3,2},{4,5},{5,4},{6,7},{7,6},{8,9},{9,8},{10,11... | collective-permute-start | bytes 393224 | tf_op jit(solution)/shard_map/ppermute | solution.py:620
  49.4 4.9 %collective-permute-start.10 = (bf16[192,256]{1,0:T(8,128)(2,1)S(1)}, bf16[192,256]{1,0:T(8,128)(2,1)S(1)}, u32[]{:S(2)}, u32[]{:S(2)}) collective-permute-start(bf16[192,256]{1,0:T(8,128)(2,1)S(1)} %slice.139), channel_id=1, source_target_pairs={{0,2},{1,3},{2,0},{3,1},{4,6},{5,7},{6,4},{7,5},{8,10},{9,11},{10,... | collective-permute-start | bytes 294920 | tf_op jit(solution)/shard_map/ppermute | solution.py:642
  54.4 5.5 %collective-permute-start.11 = (bf16[320,256]{1,0:T(8,128)(2,1)S(1)}, bf16[320,256]{1,0:T(8,128)(2,1)S(1)}, u32[]{:S(2)}, u32[]{:S(2)}) collective-permute-start(bf16[320,256]{1,0:T(8,128)(2,1)S(1)} %pad_maximum_fusion.3), channel_id=1, source_target_pairs={{0,4},{4,0},{8,12},{12,8},{16,20},{20,16},{24,28},{28,24},{1,5},{5... | collective-permute-start | bytes 491528 | tf_op jit(solution)/shard_map/ppermute | solution.py:642
  60.0 4.5 %collective-permute-start.12 = (bf16[160,256]{1,0:T(8,128)(2,1)S(1)}, bf16[160,256]{1,0:T(8,128)(2,1)S(1)}, u32[]{:S(2)}, u32[]{:S(2)}) collective-permute-start(bf16[160,256]{1,0:T(8,128)(2,1)S(1)} %slice.145), channel_id=1, source_target_pairs={{0,8},{4,12},{8,0},{12,4},{16,24},{20,28},{24,16},{28,20},{1,9},{5... | collective-permute-start | bytes 245768 | tf_op jit(solution)/shard_map/ppermute | solution.py:642
  64.5 7.3 %collective-permute-start.13 = (bf16[160,256]{1,0:T(8,128)(2,1)S(1)}, bf16[160,256]{1,0:T(8,128)(2,1)S(1)}, u32[]{:S(2)}, u32[]{:S(2)}) collective-permute-start(bf16[160,256]{1,0:T(8,128)(2,1)S(1)} %add_convert_fusion.7), channel_id=1, source_target_pairs={{0,16},{4,20},{8,24},{12,28},{16,0},{20,4},{24,8},{28,12},{1,17},{... | collective-permute-start | bytes 245768 | tf_op jit(solution)/shard_map/ppermute | solution.py:642
  71.8 7.0 %collective-permute-start.14 = (bf16[512,256]{1,0:T(8,128)(2,1)S(1)}, bf16[512,256]{1,0:T(8,128)(2,1)S(1)}, u32[]{:S(2)}, u32[]{:S(2)}) collective-permute-start(bf16[512,256]{1,0:T(8,128)(2,1)S(1)} %get-tuple-element.151), channel_id=1, source_target_pairs={{0,1},{1,0},{2,3},{3,2},{4,5},{5,4},{6,7},{7,6},{8,9},{9,8},{10,11... | collective-permute-start | bytes 786440 | tf_op jit(solution)/shard_map/ppermute | solution.py:642
  71.9 4.9 %collective-permute-start.25 = (bf16[160,256]{1,0:T(8,128)(2,1)S(1)}, bf16[160,256]{1,0:T(8,128)(2,1)S(1)}, u32[]{:S(2)}, u32[]{:S(2)}) collective-permute-start(bf16[160,256]{1,0:T(8,128)(2,1)S(1)} %add_convert_fusion.6), channel_id=1, source_target_pairs={{0,8},{4,12},{8,0},{12,4},{16,24},{20,28},{24,16},{28,20},{1,9},{5... | collective-permute-start | bytes 245768 | tf_op jit(solution)/shard_map/ppermute | solution.py:642
  76.9 9.0 %collective-permute-start.26 = (bf16[320,256]{1,0:T(8,128)(2,1)S(1)}, bf16[320,256]{1,0:T(8,128)(2,1)S(1)}, u32[]{:S(2)}, u32[]{:S(2)}) collective-permute-start(bf16[320,256]{1,0:T(8,128)(2,1)S(1)} %pad_maximum_fusion.4), channel_id=1, source_target_pairs={{0,4},{4,0},{8,12},{12,8},{16,20},{20,16},{24,28},{28,24},{1,5},{5... | collective-permute-start | bytes 491528 | tf_op jit(solution)/shard_map/ppermute | solution.py:642
  78.9 6.3 %collective-permute-start.15 = (bf16[256,256]{1,0:T(8,128)(2,1)S(1)}, bf16[256,256]{1,0:T(8,128)(2,1)S(1)}, u32[]{:S(2)}, u32[]{:S(2)}) collective-permute-start(bf16[256,256]{1,0:T(8,128)(2,1)S(1)} %slice.147), channel_id=1, source_target_pairs={{0,2},{1,3},{2,0},{3,1},{4,6},{5,7},{6,4},{7,5},{8,10},{9,11},{10,... | collective-permute-start | bytes 393224 | tf_op jit(solution)/shard_map/ppermute | solution.py:642
  80.7 5.8 %collective-permute-start.21 = (bf16[128,256]{1,0:T(8,128)(2,1)S(1)}, bf16[128,256]{1,0:T(8,128)(2,1)S(1)}, u32[]{:S(2)}, u32[]{:S(2)}) collective-permute-start(bf16[128,256]{1,0:T(8,128)(2,1)S(1)} %get-tuple-element.168), channel_id=1, source_target_pairs={{0,16},{4,20},{8,24},{12,28},{16,0},{20,4},{24,8},{28,12},{1,17},{... | collective-permute-start | bytes 196616 | tf_op jit(solution)/shard_map/ppermute | solution.py:642
  85.3 4.3 %collective-permute-start.16 = (bf16[128,256]{1,0:T(8,128)(2,1)S(1)}, bf16[128,256]{1,0:T(8,128)(2,1)S(1)}, u32[]{:S(2)}, u32[]{:S(2)}) collective-permute-start(bf16[128,256]{1,0:T(8,128)(2,1)S(1)} %slice.149), channel_id=1, source_target_pairs={{0,4},{4,0},{8,12},{12,8},{16,20},{20,16},{24,28},{28,24},{1,5},{5... | collective-permute-start | bytes 196616 | tf_op jit(solution)/shard_map/ppermute | solution.py:642
  85.9 17.2 %collective-permute-start.27 = (bf16[640,256]{1,0:T(8,128)(2,1)S(1)}, bf16[640,256]{1,0:T(8,128)(2,1)S(1)}, u32[]{:S(2)}, u32[]{:S(2)}) collective-permute-start(bf16[640,256]{1,0:T(8,128)(2,1)S(1)} %pad_maximum_fusion.1), channel_id=1, source_target_pairs={{0,2},{1,3},{2,0},{3,1},{4,6},{5,7},{6,4},{7,5},{8,10},{9,11},{10,... | collective-permute-start | bytes 983048 | tf_op jit(solution)/shard_map/ppermute | solution.py:642
  90.0 4.8 %collective-permute-start.22 = (bf16[128,256]{1,0:T(8,128)(2,1)S(1)}, bf16[128,256]{1,0:T(8,128)(2,1)S(1)}, u32[]{:S(2)}, u32[]{:S(2)}) collective-permute-start(bf16[128,256]{1,0:T(8,128)(2,1)S(1)} %pad_maximum_fusion.9), channel_id=1, source_target_pairs={{0,8},{4,12},{8,0},{12,4},{16,24},{20,28},{24,16},{28,20},{1,9},{5... | collective-permute-start | bytes 196616 | tf_op jit(solution)/shard_map/ppermute | solution.py:642
  93.6 4.9 %collective-permute-start.18 = (bf16[64,256]{1,0:T(8,128)(2,1)S(1)}, bf16[64,256]{1,0:T(8,128)(2,1)S(1)}, u32[]{:S(2)}, u32[]{:S(2)}) collective-permute-start(bf16[64,256]{1,0:T(8,128)(2,1)S(1)} %add_convert_fusion.10), channel_id=1, source_target_pairs={{0,16},{4,20},{8,24},{12,28},{16,0},{20,4},{24,8},{28,12},{1,17},{... | collective-permute-start | bytes 98312 | tf_op jit(solution)/shard_map/ppermute | solution.py:642
  98.9 4.4 %collective-permute-start.23 = (bf16[128,256]{1,0:T(8,128)(2,1)S(1)}, bf16[128,256]{1,0:T(8,128)(2,1)S(1)}, u32[]{:S(2)}, u32[]{:S(2)}) collective-permute-start(bf16[128,256]{1,0:T(8,128)(2,1)S(1)} %pad_maximum_fusion.10), channel_id=1, source_target_pairs={{0,4},{4,0},{8,12},{12,8},{16,20},{20,16},{24,28},{28,24},{1,5},{5... | collective-permute-start | bytes 196616 | tf_op jit(solution)/shard_map/ppermute | solution.py:642
  102.6 4.3 %collective-permute-start.20 = (bf16[128,256]{1,0:T(8,128)(2,1)S(1)}, bf16[128,256]{1,0:T(8,128)(2,1)S(1)}, u32[]{:S(2)}, u32[]{:S(2)}) collective-permute-start(bf16[128,256]{1,0:T(8,128)(2,1)S(1)} %pad_maximum_fusion.8), channel_id=1, source_target_pairs={{0,4},{4,0},{8,12},{12,8},{16,20},{20,16},{24,28},{28,24},{1,5},{5... | collective-permute-start | bytes 196616 | tf_op jit(solution)/shard_map/ppermute | solution.py:642
  103.2 8.7 %collective-permute-start.28 = (bf16[1280,256]{1,0:T(8,128)(2,1)S(1)}, bf16[1280,256]{1,0:T(8,128)(2,1)S(1)}, u32[]{:S(2)}, u32[]{:S(2)}) collective-permute-start(bf16[1280,256]{1,0:T(8,128)(2,1)S(1)} %pad_maximum_fusion.mine.node_mine), channel_id=1, source_target_pairs={{0,1},{1,0},{2,3},{3,2},{4,5},{5,4},{6,7},{7,6},{8,9},{9,8},{10,11... | collective-permute-start | bytes 1966088 | tf_op jit(solution)/shard_map/ppermute | solution.py:642
  106.8 5.0 %collective-permute-start.24 = (bf16[256,256]{1,0:T(8,128)(2,1)S(1)}, bf16[256,256]{1,0:T(8,128)(2,1)S(1)}, u32[]{:S(2)}, u32[]{:S(2)}) collective-permute-start(bf16[256,256]{1,0:T(8,128)(2,1)S(1)} %pad_maximum_fusion.5), channel_id=1, source_target_pairs={{0,2},{1,3},{2,0},{3,1},{4,6},{5,7},{6,4},{7,5},{8,10},{9,11},{10,... | collective-permute-start | bytes 393224 | tf_op jit(solution)/shard_map/ppermute | solution.py:642
  (20 other events, 104.7 us)
where the time goes:
time: 116 us
  Pallas kernels  41.8 us (36%)
  waiting for transfers between devices  38.4 us (33%)
  starting transfers between devices  31.5 us (27%)
  between operations  2.07 us (2%)
  local copies, waits for them, and re-layouts  1.88 us (2%)
    pallas_call x15, Pallas kernels, call(): kernel_call(kernel, micros, limit, out_shape=outs, in_specs=in_specs, out...  41.8 us
    ppermute x24, waiting for transfers between devices, flip(): return lax.ppermute(value, axis, [(i, i ^ 1 << bit) for i in range(size)])  31.7 us
    ppermute x24, starting transfers between devices, flip(): return lax.ppermute(value, axis, [(i, i ^ 1 << bit) for i in range(size)])  28.1 us
    ppermute x2, waiting for transfers between devices, turn_chip(): lax.ppermute(value, 'grp', [(i, (i + 2 * places) % groups) for i in range...  4.03 us
    ppermute x2, starting transfers between devices, turn_chip(): lax.ppermute(value, 'grp', [(i, (i + 2 * places) % groups) for i in range...  3.17 us
    ppermute x4, waiting for transfers between devices, swap_core(): return lax.ppermute(value, 'grp', [(i, i ^ 1) for i in range(groups)])  2.66 us
  transfers between devices with their start and end apart: 30, of which 16 were waited for; matrix products, arithmetic and copies ran while one was open for 0% of the time, Pallas kernels for 23%

commit v1 on v0

v1 whole, which is shorter than its diff:
```python
import functools

import jax
import jax.numpy as jnp
from jax import lax
from jax.experimental import pallas as pl
from jax.experimental.pallas import tpu as pltpu
from jax.sharding import PartitionSpec as P

F32 = jnp.float32
BF16 = jnp.bfloat16
ROWS = 128
MIB = 1024 * 1024
CHUNK = 64
I16 = jnp.int16


def mm(a, b):
    return lax.dot_general(a, b, (((1,), (0,)), ((), ())), preferred_element_type=F32)


def mm_nt(a, b):
    return lax.dot_general(a, b, (((1,), (1,)), ((), ())), preferred_element_type=F32)


def mm_tn(a, b):
    return lax.dot_general(a, b, (((0,), (0,)), ((), ())), preferred_element_type=F32)


def column(row):
    return jnp.broadcast_to(row, (128, row.shape[1])).T.astype(I16)


def flags(mask):
    return jnp.where(mask, jnp.ones((), BF16), jnp.zeros((), BF16))


def pick_rows(rows, width):
    lane = lax.broadcasted_iota(jnp.int32, (rows[0].shape[1], 128), 1).astype(I16)
    out = []
    for row in rows:
        index = column(row)
        out.append(
            jnp.concatenate([flags(index == lane + I16(128 * k)) for k in range(width // 128)], axis=1)
        )
    return out[0] if len(out) == 1 else jnp.concatenate(out, axis=0)


def pick_columns(rows, height):
    sub = lax.broadcasted_iota(jnp.int32, (height, rows[0].shape[1]), 0).astype(I16)
    out = []
    for row in rows:
        index = jnp.broadcast_to(row, (16, row.shape[1])).astype(I16)
        out.append(flags(sub == jnp.broadcast_to(index[0:1, :], sub.shape)))
    return out[0] if len(out) == 1 else jnp.concatenate(out, axis=1)


def gate(hidden):
    return 0.5 + 0.5 * jnp.tanh(0.5 * hidden)


def normalise(values):
    centre = values - jnp.mean(values, axis=-1, keepdims=True)
    spread = jnp.mean(centre * centre, axis=-1, keepdims=True)
    scale = lax.rsqrt(spread + 1e-05)
    return centre * scale, scale


def normalise_back(grad, unit, scale):
    along = jnp.mean(grad * unit, axis=-1, keepdims=True)
    return scale * (grad - jnp.mean(grad, axis=-1, keepdims=True) - unit * along)


def kernel_call(kernel, micros, limit, **kwargs):
    return pl.pallas_call(
        kernel,
        compiler_params=pltpu.CompilerParams(vmem_limit_bytes=limit * MIB),
        cost_estimate=pl.CostEstimate(
            flops=int(micros * 1.1e9), bytes_accessed=1 << 20, transcendentals=0
        ),
        **kwargs,
    )


def smem():
    return pl.BlockSpec(memory_space=pltpu.SMEM)


def whole(array):
    return pl.BlockSpec(array.shape, lambda t: (0,) * len(array.shape))


def by_tile(rows, columns):
    return pl.BlockSpec((rows, columns), lambda t: (t, 0))


def shape(rows, columns, dtype=BF16):
    return jax.ShapeDtypeStruct((rows, columns), dtype)


def chunks(total):
    return [slice(r, r + CHUNK) for r in range(0, total, CHUNK)]


def spans(start, size, tile):
    return [
        (
            slice(at, at + tile),
            slice(start + at, start + at + tile),
            slice((start + at) // tile * ROWS, ((start + at) // tile + 1) * ROWS),
        )
        for at in range(0, size, tile)
    ]


def at(start, here):
    return slice(start + here.start, start + here.stop)


def staggered(count, *stages):
    for t in range(count + len(stages) - 1):
        for k, stage in enumerate(stages):
            if 0 <= t - k < count:
                stage(t - k)


def my_core():
    return lax.rem(lax.axis_index("grp"), 2)


def split_halves(ref, mine_out, other_out):
    half = mine_out.shape[0]
    core = my_core()
    mine_out[...] = ref[pl.ds(core * half, half), :]
    other_out[...] = ref[pl.ds((1 - core) * half, half), :]


def one_hot_kernel(tile, node_count, slots, count, senders, receivers, far_out, rows_out, columns_out):
    lane = lax.broadcasted_iota(jnp.int32, (1, 128), 1)
    mask = lax.axis_index("dom") * slots
    for j in range(senders.shape[0]):
        here = slice(j * 128, (j + 1) * 128)
        row = jnp.bitwise_xor(senders[j : j + 1, :] - node_count, mask)
        far_out[here, :] = pick_rows([row], far_out.shape[1])
        row = receivers[j : j + 1, :] - j * 128 // tile * ROWS
        row = jnp.where(lane + j * 128 % tile < count[0], row, -1)
        rows_out[here, :] = pick_rows([row], ROWS)
        columns_out[:, here] = pick_columns([row], ROWS)


def sender_kernel(node_count, slots, senders, columns_out):
    mask = lax.axis_index("dom") * slots
    for j in range(senders.shape[0]):
        row = senders[j : j + 1, :]
        row = jnp.where(
            row < node_count, row, jnp.bitwise_xor(row - node_count, mask) + node_count
        )
        columns_out[:, j * 128 : (j + 1) * 128] = pick_columns([row], columns_out.shape[0])


def send_kernel(nodes, halo, near_out, far_out):
    doms, slots = halo.shape
    me = lax.axis_index("dom")
    for first, out in ((0, near_out), (doms // 2, far_out)):
        picks = [
            pick_rows([halo[pl.ds(jnp.bitwise_xor(me, first + r), 1), :]], nodes.shape[0])
            for r in range(doms // 2)
        ]
        out[...] = mm(jnp.concatenate(picks, axis=0), nodes[...]).astype(BF16)


def gather_slots(places, refs, out):
    slots = out.shape[0] // len(places)
    for r, (which, slot) in enumerate(places):
        out[r * slots : (r + 1) * slots, :] = refs[which][slot * slots : (slot + 1) * slots, :]


def group_sums(aggregates, values, mine_out, other_out, sums):
    rows = [aggregates[k : k + 1, :] for k in range(aggregates.shape[0])]
    sums[...] = mm(pick_columns(rows, sums.shape[0]), values).astype(BF16)
    split_halves(sums, mine_out, other_out)


def cotangent_kernel(aggregates, cotangent, mine_out, other_out, sums):
    group_sums(aggregates, cotangent[...], mine_out, other_out, sums)


def fine_local_kernel(
    tile, step_edges, edges, senders, recv_rows, nodes, weights,
    partial_out, send_proj, recv_proj, pick,
):
    width = nodes.shape[1]
    parts = step_edges // 128
    send_proj[...] = mm(nodes[...], weights[width : 2 * width, :]).astype(BF16)
    recv_proj[...] = mm(nodes[...], weights[2 * width : 3 * width, :]).astype(BF16)

    def choose(i):
        for j in range(parts):
            row = senders[i * parts + j : i * parts + j + 1, :]
            pick[i % 2, j * 128 : (j + 1) * 128, :] = pick_rows([row], nodes.shape[0])

    def multiply(i):
        for here, there, own in spans(i * step_edges, step_edges, tile):
            partial_out[there, :] = (
                mm(edges[there, :], weights[:width, :])
                + mm(recv_rows[there, :], recv_proj[own, :])
                + mm(pick[i % 2, here, :], send_proj[...])
            ).astype(BF16)

    staggered(edges.shape[0] // step_edges, choose, multiply)


def activate(hidden, active_out, slope_out, here):
    opened = gate(hidden)
    active = hidden * opened
    active_out[here, :] = active.astype(BF16)
    slope_out[here, :] = (opened + active * (1.0 - opened)).astype(BF16)


def fine_halo_kernel(
    tile, step_edges, places, partial, far_rows, recv_columns, aggregates, nodes, weights, *refs
):
    pieces = refs[: -(13 + 4)]
    (
        active_out, slope_out, unit_out, scale_out,
        node_active_out, node_slope_out, node_unit_out, node_scale_out, summed_out, refined_out,
        mine_out, other_out, halo,
        halo_proj, wide, wide_next, sums,
    ) = refs[-(13 + 4) :]
    node_count, width = nodes.shape
    gather_slots(places, pieces, halo)
    halo_proj[...] = mm(halo[...], weights[width : 2 * width, :]).astype(BF16)

    def first(i):
        start = i * step_edges
        wide[i % 2] = mm(far_rows[start : start + step_edges, :], halo_proj[...])
        for here in chunks(step_edges):
            there = at(start, here)
            activate(
                partial[there, :].astype(F32) + wide[i % 2, here, :], active_out, slope_out, there
            )

    def second(i):
        start = i * step_edges
        wide_next[i % 2] = mm(
            active_out[start : start + step_edges, :], weights[3 * width : 4 * width, :]
        )
        for here in chunks(step_edges):
            there = at(start, here)
            unit, scale = normalise(wide_next[i % 2, here, :])
            unit_out[there, :] = unit.astype(BF16)
            scale_out[there, :] = scale
        for here, there, own in spans(start, step_edges, tile):
            summed_out[own, :] = mm(recv_columns[:, there], unit_out[there, :]).astype(BF16)

    staggered(partial.shape[0] // step_edges, first, second)

    wide[0] = mm(nodes[...], weights[4 * width : 5 * width, :]) + mm(
        summed_out[...], weights[5 * width : 6 * width, :]
    )
    for here in chunks(node_count):
        activate(wide[0, here, :], node_active_out, node_slope_out, here)
    wide_next[0] = mm(node_active_out[...], weights[6 * width :, :])
    for here in chunks(node_count):
        unit, scale = normalise(wide_next[0, here, :])
        node_unit_out[here, :] = unit.astype(BF16)
        node_scale_out[here, :] = scale
        refined_out[here, :] = (nodes[here, :].astype(F32) + unit).astype(BF16)
    group_sums(aggregates, refined_out[...], mine_out, other_out, sums)


def coarse_pre_kernel(
    groups, edges, senders, receivers, weights,
    partial_out, send_rows_out, send_columns_out, recv_rows_out, recv_columns_out,
):
    total, width = edges.shape
    group_rows = send_columns_out.shape[0]
    tile = total // groups
    partial_out[...] = mm(edges[...], weights[:width, :]).astype(BF16)

    def run(i, carry):
        for j in range(tile // 128):
            at = i * (tile // 128) + j
            there = pl.ds(pl.multiple_of(at * 128, 128), 128)
            send, recv = senders[pl.ds(at, 1), :], receivers[pl.ds(at, 1), :]
            send_rows_out[there, :] = pick_rows([send], group_rows)
            recv_rows_out[there, :] = pick_rows([recv], ROWS)
            send_columns_out[:, there] = pick_columns([send], group_rows)
            recv_columns_out[:, there] = pick_columns([recv], ROWS)
        return carry

    lax.fori_loop(0, groups, run, 0)


def coarse_kernel(
    groups, chunk,
    table_mine, table_other, cot_mine, cot_other, partial, send_rows, send_columns, recv_rows,
    recv_columns, weights,
    table, output_out, grad_out, summed, node_active, node_pre, node_hidden_grad, send_total,
    recv_sum, active_all, hidden_grad_all, pre_all,
    cot, send_proj, recv_proj, summed_grad, node_slope, node_unit,
    slope_all, unit_all, scale_all, wide, wide_next, own_grad, send_sum,
):
    group_rows, width = table.shape
    half = group_rows // 2
    total = partial.shape[0]
    tile = total // groups
    spans = chunk // tile
    steps = total // chunk
    core = my_core()
    mine = pl.ds(core * half, half)
    other = pl.ds((1 - core) * half, half)
    table[mine, :] = table_mine[...]
    table[other, :] = table_other[...]
    cot[mine, :] = cot_mine[...]
    cot[other, :] = cot_other[...]
    send_proj[...] = mm(table[...], weights[width : 2 * width, :]).astype(BF16)
    recv_proj[...] = mm(table[...], weights[2 * width : 3 * width, :]).astype(BF16)

    def places(i):
        start = i * chunk
        return [
            (
                slice(s * tile, (s + 1) * tile),
                pl.ds(start + s * tile, tile),
                pl.ds((i * spans + s) * ROWS, ROWS),
            )
            for s in range(spans)
        ]

    for i in range(steps):
        start = i * chunk
        all_here = slice(start, start + chunk)
        for here, there, own in places(i):
            wide[here, :] = mm(send_rows[there, :], send_proj[...]) + mm(
                recv_rows[there, :], recv_proj[own, :]
            )
        for here in chunks(chunk):
            there = slice(start + here.start, start + here.stop)
            activate(
                wide[here, :] + partial[there, :].astype(F32), active_all, slope_all, there
            )
        wide_next[...] = mm(active_all[all_here, :], weights[3 * width : 4 * width, :])
        for here in chunks(chunk):
            there = slice(start + here.start, start + here.stop)
            unit, scale = normalise(wide_next[here, :])
            unit_all[there, :] = unit.astype(BF16)
            scale_all[there, :] = scale
        for here, there, own in places(i):
            summed[own, :] = mm(recv_columns[:, there], unit_all[there, :]).astype(BF16)

    nodes_here = slice(0, group_rows)
    wide[nodes_here, :] = mm(table[...], weights[4 * width : 5 * width, :]) + mm(
        summed[...], weights[5 * width : 6 * width, :]
    )
    for here in chunks(group_rows):
        activate(wide[here, :], node_active, node_slope, here)
    wide_next[nodes_here, :] = mm(node_active[...], weights[6 * width :, :])
    for here in chunks(group_rows):
        unit, scale = normalise(wide_next[here, :])
        output_out[here, :] = (table[here, :].astype(F32) + unit).astype(BF16)
        node_pre[here, :] = normalise_back(cot[here, :].astype(F32), unit, scale).astype(BF16)
    wide[nodes_here, :] = mm_nt(node_pre[...], weights[6 * width :, :])
    for here in chunks(group_rows):
        node_hidden_grad[here, :] = (wide[here, :] * node_slope[here, :].astype(F32)).astype(BF16)
    summed_grad[...] = mm_nt(
        node_hidden_grad[...], weights[5 * width : 6 * width, :]
    ).astype(BF16)
    own_grad[...] = mm_nt(node_hidden_grad[...], weights[4 * width : 5 * width, :])

    for i in range(steps):
        start = i * chunk
        all_here = slice(start, start + chunk)
        for here, there, own in places(i):
            wide[here, :] = mm(recv_rows[there, :], summed_grad[own, :])
        for here in chunks(chunk):
            there = slice(start + here.start, start + here.stop)
            pre_all[there, :] = normalise_back(
                wide[here, :], unit_all[there, :].astype(F32), scale_all[there, :]
            ).astype(BF16)
        wide_next[...] = mm_nt(pre_all[all_here, :], weights[3 * width : 4 * width, :])
        for here in chunks(chunk):
            there = slice(start + here.start, start + here.stop)
            hidden_grad_all[there, :] = (
                wide_next[here, :] * slope_all[there, :].astype(F32)
            ).astype(BF16)
        for here, there, own in places(i):
            recv_sum[own, :] = mm(recv_columns[:, there], hidden_grad_all[there, :]).astype(BF16)
        sent = mm(send_columns[:, all_here], hidden_grad_all[all_here, :])
        if i == 0:
            send_sum[...] = sent
        else:
            send_sum[...] += sent

    send_total[...] = send_sum[...].astype(BF16)
    grad_out[...] = (
        cot[...].astype(F32)
        + own_grad[...]
        + mm_nt(send_total[...], weights[width : 2 * width, :])
        + mm_nt(recv_sum[...], weights[2 * width : 3 * width, :])
    ).astype(BF16)


def coarse_products_kernel(
    groups, edges, table, summed, node_active, node_pre, node_hidden_grad, send_total, recv_total,
    active_all, hidden_grad_all, pre_all,
    weight_mine, weight_other,
    weight_all,
):
    width = table.shape[1]
    share = weight_mine.shape[0] * 2
    begin = (my_core() * (groups // 2) + lax.axis_index("grp") // 2) * share
    products = [
        (edges, hidden_grad_all),
        (table, send_total),
        (table, recv_total),
        (active_all, pre_all),
        (table, node_hidden_grad),
        (summed, node_hidden_grad),
        (node_active, node_pre),
    ]
    for b, (left, right) in enumerate(products):

        @pl.when((b * width < begin + share) & ((b + 1) * width > begin))
        def _():
            weight_all[b * width : (b + 1) * width, :] = mm_tn(left[...], right[...])

    chunk_rows = share // 4
    place = coarse_place()
    for r in range(4):
        first = pl.multiple_of(begin + jnp.bitwise_xor(place, r) * chunk_rows, 8)
        out = (weight_mine, weight_other)[r // 2]
        here = slice((r % 2) * chunk_rows, (r % 2 + 1) * chunk_rows)
        out[here, :] = weight_all[pl.ds(first, chunk_rows), :].astype(BF16)


def coarse_place():
    dom = lax.axis_index("dom")
    return lax.rem(dom, 2) * 2 + lax.rem(dom // 2, 2)


def fine_place():
    grp = lax.axis_index("grp")
    return lax.rem(grp, 2) * 8 + lax.rem(grp // 2, 2) * 4 + coarse_place()


def node_back_kernel(
    aggregates, table_grad, cotangent, node_active, node_slope, node_unit, node_scale, summed,
    nodes, weights,
    node_grad_out, summed_grad_out, weight_out,
    pre, hidden_grad, wide, wide_next,
):
    node_count, width = nodes.shape
    rows = [aggregates[k : k + 1, :] for k in range(aggregates.shape[0])]
    wide[...] = mm(pick_rows(rows, table_grad.shape[0]), table_grad[...])
    for here in chunks(node_count):
        grad = (cotangent[here, :].astype(F32) + 0.125 * wide[here, :]).astype(BF16)
        grad = grad.astype(F32)
        node_grad_out[here, :] = grad
        pre[here, :] = normalise_back(
            grad, node_unit[here, :].astype(F32), node_scale[here, :]
        ).astype(BF16)
    wide_next[...] = mm_nt(pre[...], weights[6 * width :, :])
    for here in chunks(node_count):
        hidden_grad[here, :] = (
            wide_next[here, :] * node_slope[here, :].astype(F32)
        ).astype(BF16)
    summed_grad_out[...] = mm_nt(
        hidden_grad[...], weights[5 * width : 6 * width, :]
    ).astype(BF16)
    node_grad_out[...] += mm_nt(hidden_grad[...], weights[4 * width : 5 * width, :])
    weight_out[:width, :] = mm_tn(nodes[...], hidden_grad[...]).astype(BF16)
    weight_out[width : 2 * width, :] = mm_tn(summed[...], hidden_grad[...]).astype(BF16)
    weight_out[2 * width :, :] = mm_tn(node_active[...], pre[...]).astype(BF16)


def edge_back_kernel(
    tile, step_edges, edges, active, slope, unit, scale, send_columns, recv_rows, recv_columns,
    summed_grad, weights, nodes, halo, node_weights,
    hidden_grad_out, near_out, recv_sum, weight_mine, weight_other, halo_near, halo_far,
    pre, wide, wide_next, weight_all,
):
    node_count, width = nodes.shape

    def first(i):
        start = i * step_edges
        for here, there, own in spans(start, step_edges, tile):
            wide[i % 2, here, :] = mm(recv_rows[there, :], summed_grad[own, :])
        for here in chunks(step_edges):
            there = at(start, here)
            pre[there, :] = normalise_back(
                wide[i % 2, here, :], unit[there, :].astype(F32), scale[there, :]
            ).astype(BF16)

    def second(i):
        start = i * step_edges
        wide_next[i % 2] = mm_nt(
            pre[start : start + step_edges, :], weights[3 * width : 4 * width, :]
        )
        for here in chunks(step_edges):
            there = at(start, here)
            hidden_grad_out[there, :] = (
                wide_next[i % 2, here, :] * slope[there, :].astype(F32)
            ).astype(BF16)

    staggered(edges.shape[0] // step_edges, first, second)

    hidden_grad = hidden_grad_out[...]
    near_out[...] = mm(send_columns[:node_count, :], hidden_grad).astype(BF16)
    far = mm(send_columns[node_count:, :], hidden_grad).astype(BF16)
    for here, there, own in spans(0, edges.shape[0], tile):
        recv_sum[own, :] = mm(recv_columns[:, there], hidden_grad_out[there, :]).astype(BF16)
    weight_all[3 * width : 4 * width, :] = mm_tn(active[...], pre[...])
    weight_all[:width, :] = mm_tn(edges[...], hidden_grad)
    weight_all[width : 2 * width, :] = mm_tn(nodes[...], near_out[...]) + mm_tn(halo[...], far)
    weight_all[2 * width : 3 * width, :] = mm_tn(nodes[...], recv_sum[...])
    weight_all[4 * width :, :] = node_weights[...].astype(F32)
    far_half = far.shape[0] // 2
    send_weights = weights[width : 2 * width, :]
    halo_near[...] = mm_nt(far[:far_half, :], send_weights).astype(BF16)
    halo_far[...] = mm_nt(far[far_half:, :], send_weights).astype(BF16)
    rows = weight_all.shape[0] // 16
    place = fine_place()
    for r in range(16):
        begin = pl.multiple_of(jnp.bitwise_xor(place, r) * rows, 16)
        out = (weight_mine, weight_other)[r // 8]
        out[(r % 8) * rows : (r % 8 + 1) * rows, :] = weight_all[pl.ds(begin, rows), :].astype(
            BF16
        )


def edge_out_kernel(hidden_grad, weights, edge_grad_out):
    edge_grad_out[...] = mm_nt(hidden_grad[...], weights[: hidden_grad.shape[1], :]).astype(BF16)


def fine_out_kernel(aggregates, table, refined, fine_out):
    rows = [aggregates[k : k + 1, :] for k in range(aggregates.shape[0])]
    lifted = mm(pick_rows(rows, table.shape[0]), table[...])
    fine_out[...] = (refined[...].astype(F32) + lifted).astype(BF16)


def return_kernel(places, halo, node_grad, near, recv_total, weights, *refs):
    doms = len(places)
    pieces, out, values = refs[:-2], refs[-2], refs[-1]
    width = out.shape[1]
    me = lax.axis_index("dom")
    gather_slots(places, pieces, values)
    row = jnp.concatenate(
        [halo[pl.ds(jnp.bitwise_xor(me, r), 1), :] for r in range(doms)], axis=1
    )
    parts = [row[:, 128 * k : 128 * (k + 1)] for k in range(row.shape[1] // 128)]
    out[...] = (
        node_grad[...]
        + mm(pick_columns(parts, out.shape[0]), values[...])
        + mm_nt(near[...], weights[width : 2 * width, :])
        + mm_nt(recv_total[...], weights[2 * width : 3 * width, :])
    ).astype(BF16)


def coarse_final_kernel(chips, scale, mine, other, out):
    share = mine.shape[0] // chips
    rows = share // 4
    core = my_core()
    chip = lax.axis_index("grp") // 2
    place = coarse_place()
    for k in range(chips):
        at = lax.rem(chip - k + chips, chips)
        for r in range(4):
            here = slice(k * share + r * rows, k * share + (r + 1) * rows)
            inside = jnp.bitwise_xor(place, r) * rows
            first = pl.multiple_of((core * chips + at) * share + inside, 8)
            second = pl.multiple_of(((1 - core) * chips + at) * share + inside, 8)
            out[pl.ds(first, rows), :] = mine[here, :].astype(F32) * scale
            out[pl.ds(second, rows), :] = other[here, :].astype(F32) * scale


def fine_final_kernel(scale, mine, other, out):
    rows = out.shape[0] // 16
    place = fine_place()
    for r in range(16):
        first = pl.multiple_of(jnp.bitwise_xor(place, r) * rows, 16)
        here = slice((r % 8) * rows, (r % 8 + 1) * rows)
        out[pl.ds(first, rows), :] = (mine, other)[r // 8][here, :].astype(F32) * scale


def swap_core(value, groups):
    return lax.ppermute(value, "grp", [(i, i ^ 1) for i in range(groups)])


def turn_chip(value, groups, places):
    return lax.ppermute(
        value, "grp", [(i, (i + 2 * places) % groups) for i in range(groups)]
    )


def group_rest(own, scale, groups):
    sent = own.astype(BF16)
    for k in range(1, groups // 2):
        own = own + turn_chip(sent, groups, k).astype(F32)
    return (own * scale).astype(BF16)


def pair_sum(mine, other, groups):
    return mine.astype(F32) + swap_core(other, groups).astype(F32)


def flip(value, axis, bit):
    size = lax.axis_size(axis)
    return lax.ppermute(value, axis, [(i, i ^ (1 << bit)) for i in range(size)])


def after(value, *others):
    return lax.optimization_barrier((value, *others))[0]


def add(a, b):
    return (a.astype(F32) + b.astype(F32)).astype(BF16)


def halved(values):
    half = values.shape[0] // 2
    return values[:half], values[half:]


def exchange_slots(near, far, slots, ties=()):
    doms = lax.axis_size("dom")
    arrays = [near]
    places = [(0, r) for r in range(doms // 2)] + [None] * (doms // 2)
    for bit in reversed(range(doms.bit_length() - 1)):
        moved_slots = [r for r in range(doms) if r >> bit & 1]
        if bit == doms.bit_length() - 2:
            sent = far
        else:
            sent = jnp.concatenate(
                [arrays[w][slot * slots : (slot + 1) * slots] for w, slot in
                 (places[r] for r in moved_slots)],
                axis=0,
            )
        stage = len(arrays) - 1
        if stage < len(ties):
            sent = after(sent, ties[stage])
        arrays.append(flip(sent, "dom", bit))
        for i, r in enumerate(moved_slots):
            places[r] = (len(arrays) - 1, i)
    return arrays, places


def body(
    nodes,
    edges,
    senders,
    receivers,
    edge_count,
    halo_rows,
    aggregates,
    coarse_edges,
    coarse_senders,
    coarse_receivers,
    cotangent,
    fine_weights,
    coarse_weights,
):
    node_count, width = nodes.shape
    edge_total = edges.shape[0]
    groups = lax.axis_size("grp")
    domains = lax.axis_size("dom")
    devices = groups * domains
    chips = groups // 2
    group_rows = ROWS * groups
    slots = halo_rows.shape[2]
    halo_count = domains * slots
    coarse_total = coarse_senders.shape[1]
    tiles = node_count // ROWS
    tile = edge_total // tiles
    step_edges = 2 * tile
    steps = tiles // 2

    halo_index = halo_rows[0]
    sender_rows = senders.reshape(-1, 128)
    receiver_rows = receivers.reshape(-1, 128)
    aggregate_rows = aggregates.reshape(-1, 128)
    half = shape(group_rows // 2, width)

    def call(kernel, name, micros, outs, ins, scratch=(), limit=20, specs=None, grid=None):
        outs = tuple(outs)
        in_specs, out_specs = specs or (
            [
                smem() if len(leaf.shape) == 1 else pl.BlockSpec(memory_space=pltpu.VMEM)
                for leaf in ins
            ],
            [pl.BlockSpec(memory_space=pltpu.VMEM) for leaf in outs],
        )
        result = kernel_call(
            kernel,
            micros,
            limit,
            out_shape=outs,
            in_specs=in_specs,
            out_specs=out_specs,
            scratch_shapes=list(scratch),
            name=name,
            **({} if grid is None else {"grid": (grid,)}),
        )(*ins)
        return result[0] if len(outs) == 1 else result

    def streamed(kernel, name, micros, outs, ins, scratch=(), limit=20):
        specs = ([whole(leaf) for leaf in ins], [whole(leaf) for leaf in outs])
        return call(kernel, name, micros, outs, ins, scratch, limit, specs, 1)

    def room(rows, columns=width, dtype=BF16):
        return pltpu.VMEM((rows, columns), dtype)

    send_near, send_far = streamed(
        send_kernel, "send_rows", 2,
        [shape(halo_count // 2, width), shape(halo_count // 2, width)], [nodes, halo_index],
    )
    send_far, later_cotangent = lax.optimization_barrier((send_far, cotangent))
    incoming, places = exchange_slots(send_near, send_far, slots)
    cot_mine, cot_other = call(
        cotangent_kernel, "cotangent_sums", 1, [half, half], [aggregate_rows, later_cotangent],
        scratch=[room(group_rows)],
    )
    cot_pair = pair_sum(cot_mine, cot_other, groups)
    far_rows, recv_rows, recv_columns = call(
        functools.partial(one_hot_kernel, tile, node_count, slots), "one_hots", 1,
        [
            shape(edge_total, halo_count), shape(edge_total, ROWS), shape(ROWS, edge_total),
        ],
        [edge_count, after(sender_rows, cot_mine), receiver_rows],
    )

    partial = call(
        functools.partial(fine_local_kernel, tile, step_edges), "fine_local", 5,
        [shape(edge_total, width)],
        [edges, sender_rows, recv_rows, nodes, after(fine_weights, incoming[1])],
        scratch=[
            room(node_count), room(node_count), pltpu.VMEM((2, step_edges, node_count), BF16)
        ],
        limit=24,
    )
    partial, cot_pair = lax.optimization_barrier((partial, cot_pair))
    cot_own = group_rest(cot_pair, 1.0, groups)
    per_edge = shape(edge_total, width)
    per_node = shape(node_count, width)
    halo_outs = [
        per_edge, per_edge, per_edge, shape(edge_total, 1, F32), per_node, per_node, per_node,
        shape(node_count, 1, F32), per_node, per_node, half, half, shape(halo_count, width),
    ]
    two_steps = pltpu.VMEM((2, step_edges, width), F32)
    (
        active, slope, unit, scale, node_active, node_slope, node_unit, node_scale, summed,
        refined, part_mine, part_other, halo_nodes,
    ) = call(
        functools.partial(fine_halo_kernel, tile, step_edges, places), "fine_halo", 6, halo_outs,
        [partial, far_rows, recv_columns, aggregate_rows, nodes, fine_weights, *incoming],
        scratch=[room(halo_count), two_steps, two_steps, room(group_rows)],
        limit=24,
    )
    part_mine, part_other, cot_own = lax.optimization_barrier((part_mine, part_other, cot_own))
    coarse_ins = [
        coarse_edges[0], coarse_senders.reshape(-1, 128), coarse_receivers.reshape(-1, 128),
        coarse_weights,
    ]
    coarse_ins, part_other = lax.optimization_barrier((coarse_ins, part_other))
    pair = pair_sum(part_mine, part_other, groups)
    coarse_pre = call(
        functools.partial(coarse_pre_kernel, groups), "coarse_pre", 2,
        [
            shape(coarse_total, width), shape(coarse_total, group_rows),
            shape(group_rows, coarse_total), shape(coarse_total, ROWS), shape(ROWS, coarse_total),
        ],
        [after(coarse_ins[0], pair), *coarse_ins[1:]],
    )
    send_columns = call(
        functools.partial(sender_kernel, node_count, slots), "sender_one_hots", 1,
        [shape(node_count + halo_count, edge_total)], [after(sender_rows, pair)],
        limit=8,
    )
    table_own = after(group_rest(pair, 0.125, groups), coarse_pre[0], send_columns)
    tables = [table_own, swap_core(table_own, groups)]
    cots = [cot_own, swap_core(cot_own, groups)]

    coarse_chunk = 4 * coarse_total // groups
    share = 7 * width // groups
    coarse_wide = shape(coarse_total, width)
    group_wide = shape(group_rows, width)
    coarse_rows = max(coarse_chunk, group_rows)
    table, coarse_table, table_grad, *coarse_kept = call(
        functools.partial(coarse_kernel, groups, coarse_chunk), "coarse_both_ways", 8,
        [group_wide] * 9 + [coarse_wide] * 3,
        [*tables, *cots, *coarse_pre, coarse_weights],
        scratch=[room(group_rows)] * 6
        + [room(coarse_total)] * 2
        + [room(coarse_total, 1, F32)]
        + [room(coarse_rows, width, F32)] * 2
        + [room(group_rows, width, F32)] * 2,
        limit=20,
    )
    node_partial, summed_grad, node_weights = call(
        node_back_kernel, "node_back", 5,
        [shape(node_count, width, F32), per_node, shape(3 * width, width)],
        [
            aggregate_rows, table_grad, cotangent, node_active, node_slope, node_unit, node_scale,
            summed, nodes, fine_weights,
        ],
        scratch=[room(node_count)] * 2 + [room(node_count, width, F32)] * 2,
    )
    half_weights = shape(7 * width // 2, width)
    hidden_grad, near, recv_total, weight_mine, weight_other, halo_near, halo_far = call(
        functools.partial(edge_back_kernel, tile, step_edges), "edge_back", 8,
        [per_edge, per_node, per_node, half_weights, half_weights]
        + [shape(halo_count // 2, width)] * 2,
        [
            edges, active, slope, unit, scale, send_columns, recv_rows, recv_columns,
            summed_grad, fine_weights, nodes, halo_nodes, node_weights,
        ],
        scratch=[room(edge_total), two_steps, two_steps, room(7 * width, width, F32)],
        limit=20,
    )

    more_grp = range(2, groups.bit_length() - 1)
    more_dom = range(2, domains.bit_length() - 1)
    received = flip(weight_other, "grp", 0)
    coarse_mine, coarse_other = call(
        functools.partial(coarse_products_kernel, groups), "coarse_products", 1,
        [shape(share // 2, width)] * 2,
        [after(coarse_edges[0], weight_other), table, *coarse_kept],
        scratch=[room(7 * width, width, F32)],
    )
    received = after(received, coarse_mine)
    mine, other = halved(add(weight_mine, received))

    received = flip(other, "grp", 1)
    fine_out = streamed(
        fine_out_kernel, "fine_out", 2, [per_node],
        [aggregate_rows, coarse_table, after(refined, other)],
    )
    coarse_received = flip(after(coarse_other, fine_out), "dom", 0)
    ties = [fine_out]
    mine, other = halved(add(mine, received))

    received = flip(other, "dom", 0)
    coarse_mine, coarse_other = halved(add(coarse_mine, coarse_received))
    coarse_received = flip(after(coarse_other, other), "dom", 1)
    ties.append(other)
    mine, other = halved(add(mine, received))

    received = flip(other, "dom", 1)
    ties.append(other)
    returned, places_back = exchange_slots(halo_near, halo_far, slots, ties)
    coarse_own = add(coarse_mine, coarse_received)
    for bit in more_dom:
        coarse_own = add(coarse_own, flip(after(coarse_own, other), "dom", bit))
    own = add(mine, received)
    for axis, bits in (("grp", more_grp), ("dom", more_dom)):
        for bit in bits:
            own = add(own, flip(own, axis, bit))
    for bit in (1, 0):
        coarse_own = jnp.concatenate([coarse_own, flip(coarse_own, "dom", bit)], axis=0)
    coarse_mine = jnp.concatenate(
        [coarse_own] + [turn_chip(coarse_own, groups, k) for k in range(1, chips)], axis=0
    )
    weight_shape = shape(7 * width, width, F32)
    coarse_total_grad = streamed(
        functools.partial(coarse_final_kernel, chips, (coarse_total * domains) ** (-0.5)),
        "coarse_weights", 2, [weight_shape], [coarse_mine, swap_core(coarse_mine, groups)],
    )
    node_grad = streamed(
        functools.partial(return_kernel, places_back), "halo_return", 3, [per_node],
        [halo_index, node_partial, near, recv_total, fine_weights, *returned],
        scratch=[room(halo_count)],
    )
    own = jnp.concatenate([own, flip(own, "dom", 1)], axis=0)
    own = jnp.concatenate([own, flip(own, "dom", 0)], axis=0)
    edge_grad = call(
        edge_out_kernel, "edge_out", 3, [per_edge], [after(hidden_grad, own), fine_weights],
        specs=(
            [by_tile(step_edges, width), whole(fine_weights)],
            [by_tile(step_edges, width)],
        ),
        grid=steps,
    )
    received = after(flip(own, "grp", 1), node_grad, edge_grad)
    own = jnp.concatenate([own, received], axis=0)
    fine_total_grad = streamed(
        functools.partial(fine_final_kernel, (edge_total * devices) ** (-0.5)),
        "fine_weights", 2, [weight_shape], [own, flip(own, "grp", 0)],
    )
    return (fine_out, node_grad, edge_grad, fine_total_grad, coarse_total_grad)


def solution(mesh):
    placed = (
        P(("dom", "grp"), None),
        P(("dom", "grp"), None),
        P(("dom", "grp")),
        P(("dom", "grp")),
        P(("dom", "grp")),
        P(("dom", "grp"), None, None),
        P(("dom", "grp")),
        P("dom", None, None),
        P("dom", None),
        P("dom", None),
        P(("dom", "grp"), None),
        P(),
        P(),
    )
    return jax.shard_map(
        body,
        mesh=mesh,
        in_specs=placed,
        out_specs=(
            P(("dom", "grp"), None),
            P(("dom", "grp"), None),
            P(("dom", "grp"), None),
            P(),
            P(),
        ),
        check_vma=False,
    )
```

time: 116 us -> 101 us (0.87)
  waiting for transfers between devices: 38.4 us -> 21.7 us
  Pallas kernels: 41.8 us -> 40.2 us
  starting transfers between devices: 31.5 us -> 33 us
  local copies, waits for them, and re-layouts: 1.88 us -> 3.21 us
    ppermute x24 -> x20, waiting for transfers between devices: 31.7 us -> 17.1 us  [flip(): return lax.ppermute(value, axis, [(i, i ^ 1 << bit) for i in range(size)])]
    pallas_call x15 -> x16, Pallas kernels: 41.8 us -> 40.2 us  [call(): kernel_call(kernel, micros, limit, out_shape=outs, in_specs=in_specs, out...]
    ppermute x2 -> x3, waiting for transfers between devices: 4.03 us -> 2.43 us  [turn_chip(): lax.ppermute(value, 'grp', [(i, (i + 2 * places) % groups) for i in range...]
    unnamed x28 -> x52, local copies, waits for them, and re-layouts: 1.79 us -> 3.14 us
    ppermute x2 -> x3, starting transfers between devices: 3.17 us -> 4.22 us  [turn_chip(): lax.ppermute(value, 'grp', [(i, (i + 2 * places) % groups) for i in range...]
    ppermute x4 -> x5, waiting for transfers between devices: 2.66 us -> 2.17 us  [swap_core(): return lax.ppermute(value, 'grp', [(i, i ^ 1) for i in range(groups)])]
    ppermute x24 -> x20, starting transfers between devices: 28.1 us -> 28 us  [flip(): return lax.ppermute(value, axis, [(i, i ^ 1 << bit) for i in range(size)])]
  transfers between devices with their start and end apart: 30 -> 28, of which waited for: 16 -> 16; matrix products, arithmetic and copies ran while one was open for 0% -> 0% of each run, Pallas kernels for 23% -> 21%
where the time goes in v1:
time: 101 us; the launch traced here: 100 us
  Pallas kernels  40.2 us (40%)
  starting transfers between devices  33 us (33%)
  waiting for transfers between devices  21.7 us (21%)
  local copies, waits for them, and re-layouts  3.21 us (3%)
  between operations  1.79 us (2%)
    pallas_call x16, Pallas kernels, call(): kernel_call(kernel, micros, limit, out_shape=outs, in_specs=in_specs, out...  40.2 us
    ppermute x20, starting transfers between devices, flip(): return lax.ppermute(value, axis, [(i, i ^ 1 << bit) for i in range(size)])  28 us
    ppermute x20, waiting for transfers between devices, flip(): return lax.ppermute(value, axis, [(i, i ^ 1 << bit) for i in range(size)])  17.1 us
    ppermute x3, starting transfers between devices, turn_chip(): lax.ppermute(value, 'grp', [(i, (i + 2 * places) % groups) for i in range...  4.22 us
    unnamed x52, local copies, waits for them, and re-layouts  3.14 us
    ppermute x3, waiting for transfers between devices, turn_chip(): lax.ppermute(value, 'grp', [(i, (i + 2 * places) % groups) for i in range...  2.43 us
    ppermute x5, waiting for transfers between devices, swap_core(): return lax.ppermute(value, 'grp', [(i, i ^ 1) for i in range(groups)])  2.17 us
  transfers between devices with their start and end apart: 28, of which 16 were waited for; matrix products, arithmetic and copies ran while one was open for 0% of the time, Pallas kernels for 21%

profile of v1, /device:TPU:0, one launch (start us, length us, event | category | flops | bytes accessed | tf_op | source)
XLA Modules:
  0.0 100.4 jit_solution(15549337808313029965)
XLA Ops:
  2.8 4.1 %collective-permute-start = (bf16[128,256]{1,0:T(8,128)(2,1)S(1)}, bf16[128,256]{1,0:T(8,128)(2,1)S(1)}, u32[]{:S(2)}, u32[]{:S(2)}) collective-permute-start(bf16[128,256]{1,0:T(8,128)(2,1)S(1)} %get-tuple-element.87), channel_id=1, source_target_pairs={{0,16},{4,20},{8,24},{12,28},{16,0},{20,4},{24,8},{28,12},{1,17},{... | collective-permute-start | bytes 196616 | tf_op jit(solution)/shard_map/ppermute | solution.py:609
  11.3 3.7 %fine_local.1.partial = bf16[4096,256]{1,0:T(8,128)(2,1)S(1)} custom-call(bf16[4096,256]{1,0:T(8,128)(2,1)S(1)} %copy-done.2, s32[32,128]{1,0:T(8,128)S(1)} %bitcast.10, bf16[4096,128]{1,0:T(8,128)(2,1)S(1)} %get-tuple-element.86.recv_rows, bf16[1024,256]{1,0:T(8,128)(2,1)S(1)} %copy-done.7, bf16[1792,256]{1,0:T(8,128)(2,1)S(1)} %copy-done.4), custom_call_target="tpu_custom_call" | custom-call | flops 5500000256 | bytes 1048576 | tf_op jit(solution)/shard_map/fine_local/pallas_call | solution.py:693
  15.0 1.7 %collective-permute-start.3 = (bf16[128,256]{1,0:T(8,128)(2,1)S(1)}, bf16[128,256]{1,0:T(8,128)(2,1)S(1)}, u32[]{:S(2)}, u32[]{:S(2)}) collective-permute-start(bf16[128,256]{1,0:T(8,128)(2,1)S(1)} %pad_maximum_fusion.7), channel_id=1, source_target_pairs={{0,4},{4,0},{8,12},{12,8},{16,20},{20,16},{24,28},{28,24},{1,5},{5... | collective-permute-start | bytes 196616 | tf_op jit(solution)/shard_map/ppermute | solution.py:609
  16.8 1.6 %collective-permute-start.4 = (bf16[256,256]{1,0:T(8,128)(2,1)S(1)}, bf16[256,256]{1,0:T(8,128)(2,1)S(1)}, u32[]{:S(2)}, u32[]{:S(2)}) collective-permute-start(bf16[256,256]{1,0:T(8,128)(2,1)S(1)} %convert_element_type.104), channel_id=1, source_target_pairs={{0,2},{1,3},{2,0},{3,1},{4,6},{5,7},{6,4},{7,5},{8,10},{9,11},{10,... | collective-permute-start | bytes 393224 | tf_op jit(solution)/shard_map/ppermute | solution.py:591
  19.3 5.0 %fine_halo.1 = (bf16[4096,256]{1,0:T(8,128)(2,1)S(1)}, bf16[4096,256]{1,0:T(8,128)(2,1)S(1)}, bf16[4096,256]{1,0:T(8,128)(2,1)S(1)}, f32[4096,1]{1,0:T(8,128)S(1...) custom-call(bf16[4096,256]{1,0:T(8,128)(2,1)S(1)} %fine_local.1.part, ...), custom_call_target="tpu_custom_call" | custom-call | flops 6600000000 | bytes 1048576 | tf_op jit(solution)/shard_map/fine_halo/pallas_call | solution.py:693
  27.2 1.7 %collective-permute-start.6 = (bf16[256,256]{1,0:T(8,128)(2,1)S(1)}, bf16[256,256]{1,0:T(8,128)(2,1)S(1)}, u32[]{:S(2)}, u32[]{:S(2)}) collective-permute-start(bf16[256,256]{1,0:T(8,128)(2,1)S(1)} %fusion), channel_id=1, source_target_pairs={{0,2},{1,3},{2,0},{3,1},{4,6},{5,7},{6,4},{7,5},{8,10},{9,11},{10,... | collective-permute-start | bytes 393224 | tf_op jit(solution)/shard_map/ppermute | solution.py:591
  29.0 1.8 %coarse_pre.1 = (bf16[2048,256]{1,0:T(8,128)(2,1)S(1)}, bf16[2048,512]{1,0:T(8,128)(2,1)S(1)}, bf16[512,2048]{1,0:T(8,128)(2,1)S(1)}, bf16[2048,128]{1,0:T(8,128)(2,1)S(1)}, bf16[128,2048]{1,0:T(8,128)(2,1)S(1)}) custom-call(bf16[2048,256]{1,0:T(8,128)(2,1)S(1)} %bitcast.7, s32[16,128]{1,0:T(8,128)S(1)} %bitcast.13, s32[16,128]{1,0:T(8,128)S(1)} %bitcast.14, ...), custom_call_target="tpu_custom_call" | custom-call | flops 2200000000 | bytes 1048576 | tf_op jit(solution)/shard_map/coarse_pre/pallas_call | solution.py:693
  30.8 2.8 %sender_one_hots.1.send_columns = bf16[1280,4096]{1,0:T(8,128)(2,1)S(1)} custom-call(s32[32,128]{1,0:T(8,128)S(1)} %bitcast.11), custom_call_target="tpu_custom_call" | custom-call | flops 1100000000 | bytes 1048576 | tf_op jit(solution)/shard_map/sender_one_hots/pallas_call | solution.py:693
  35.1 6.1 %coarse_both_ways.1 = (bf16[512,256]{1,0:T(8,128)(2,1)S(1)}, bf16[512,256]{1,0:T(8,128)(2,1)S(1)}, bf16[512,256]{1,0:T(8,128)(2,1)S(1)}, bf16[512,256]{1,0:T(8,1...) custom-call(bf16[256,256]{1,0:T(8,128)(2,1)S(1)} %multiply_convert_f, ...), custom_call_target="tpu_custom_call" | custom-call | flops 8800000000 | bytes 1048576 | tf_op jit(solution)/shard_map/coarse_both_ways/pallas_call | solution.py:693
  41.3 2.1 %node_back.1 = (f32[1024,256]{1,0:T(8,128)S(1)}, bf16[1024,256]{1,0:T(8,128)(2,1)S(1)}, bf16[768,256]{1,0:T(8,128)(2,1)S(1)}) custom-call(s32[8,128]{1,0:T(8,128)S(1)} %bitcast.17, bf16[512,256]{1,0:T(8,128)(2,1)S(1)} %get-tuple-element.119.table_grad, bf16[1024,256]{1,0:T(8,128)(2,1)S(1)} %copy-done.5, ...), custom_call_target="tpu_custom_call" | custom-call | flops 5500000256 | bytes 1048576 | tf_op jit(solution)/shard_map/node_back/pallas_call | solution.py:693
  43.4 7.6 %edge_back.1 = (bf16[4096,256]{1,0:T(8,128)(2,1)S(1)}, bf16[1024,256]{1,0:T(8,128)(2,1)S(1)}, bf16[1024,256]{1,0:T(8,128)(2,1)S(1)}, bf16[896,256]{1,0:T(8,128)(...) custom-call(bf16[4096,256]{1,0:T(8,128)(2,1)S(1)} %copy-done.2, ...), custom_call_target="tpu_custom_call" | custom-call | flops 8800000000 | bytes 1048576 | tf_op jit(solution)/shard_map/edge_back/pallas_call | solution.py:693
  55.8 3.2 %collective-permute-start.10 = (bf16[128,256]{1,0:T(8,128)(2,1)S(1)}, bf16[128,256]{1,0:T(8,128)(2,1)S(1)}, u32[]{:S(2)}, u32[]{:S(2)}) collective-permute-start(bf16[128,256]{1,0:T(8,128)(2,1)S(1)} %get-tuple-element.149), channel_id=1, source_target_pairs={{0,16},{4,20},{8,24},{12,28},{16,0},{20,4},{24,8},{28,12},{1,17},{... | collective-permute-start | bytes 196616 | tf_op jit(solution)/shard_map/ppermute | solution.py:609
  59.9 2.7 %collective-permute-done.10.refs_1_ = bf16[128,256]{1,0:T(8,128)(2,1)S(1)} collective-permute-done((bf16[128,256]{1,0:T(8,128)(2,1)S(1)}, bf16[128,256]{1,0:T(8,128)(2,1)S(1)}, u32[]{:S(2)}, u32[]{:S(2)}) %collective-permute-start.10) | collective-permute-done | bytes 65568 | tf_op jit(solution)/shard_map/ppermute | solution.py:609
  62.6 3.5 %collective-permute-done.11 = bf16[448,256]{1,0:T(8,128)(2,1)S(1)} collective-permute-done((bf16[448,256]{1,0:T(8,128)(2,1)S(1)}, bf16[448,256]{1,0:T(8,128)(2,1)S(1)}, u32[]{:S(2)}, u32[]{:S(2)}) %collective-permute-start.11) | collective-permute-done | bytes 229408 | tf_op jit(solution)/shard_map/ppermute | solution.py:609
  67.3 1.5 %collective-permute-start.12 = (bf16[128,256]{1,0:T(8,128)(2,1)S(1)}, bf16[128,256]{1,0:T(8,128)(2,1)S(1)}, u32[]{:S(2)}, u32[]{:S(2)}) collective-permute-start(bf16[128,256]{1,0:T(8,128)(2,1)S(1)} %pad_maximum_fusion.8), channel_id=1, source_target_pairs={{0,8},{4,12},{8,0},{12,4},{16,24},{20,28},{24,16},{28,20},{1,9},{5... | collective-permute-start | bytes 196616 | tf_op jit(solution)/shard_map/ppermute | solution.py:609
  68.8 1.6 %collective-permute-done.22 = bf16[112,256]{1,0:T(8,128)(2,1)S(1)} collective-permute-done((bf16[112,256]{1,0:T(8,128)(2,1)S(1)}, bf16[112,256]{1,0:T(8,128)(2,1)S(1)}, u32[]{:S(2)}, u32[]{:S(2)}) %collective-permute-start.22) | collective-permute-done | bytes 57376 | tf_op jit(solution)/shard_map/ppermute | solution.py:609
  71.7 1.5 %collective-permute-start.15 = (bf16[112,256]{1,0:T(8,128)(2,1)S(1)}, bf16[112,256]{1,0:T(8,128)(2,1)S(1)}, u32[]{:S(2)}, u32[]{:S(2)}) collective-permute-start(bf16[112,256]{1,0:T(8,128)(2,1)S(1)} %slice.100), channel_id=1, source_target_pairs={{0,8},{4,12},{8,0},{12,4},{16,24},{20,28},{24,16},{28,20},{1,9},{5... | collective-permute-start | bytes 172040 | tf_op jit(solution)/shard_map/ppermute | solution.py:609
  76.0 1.7 %collective-permute-start.16 = (bf16[112,256]{1,0:T(8,128)(2,1)S(1)}, bf16[112,256]{1,0:T(8,128)(2,1)S(1)}, u32[]{:S(2)}, u32[]{:S(2)}) collective-permute-start(bf16[112,256]{1,0:T(8,128)(2,1)S(1)} %add_convert_fusion.8), channel_id=1, source_target_pairs={{0,16},{4,20},{8,24},{12,28},{16,0},{20,4},{24,8},{28,12},{1,17},{... | collective-permute-start | bytes 172040 | tf_op jit(solution)/shard_map/ppermute | solution.py:609
  79.3 1.9 %collective-permute-done.16 = bf16[112,256]{1,0:T(8,128)(2,1)S(1)} collective-permute-done((bf16[112,256]{1,0:T(8,128)(2,1)S(1)}, bf16[112,256]{1,0:T(8,128)(2,1)S(1)}, u32[]{:S(2)}, u32[]{:S(2)}) %collective-permute-start.16) | collective-permute-done | bytes 57376 | tf_op jit(solution)/shard_map/ppermute | solution.py:609
  81.2 2.1 %collective-permute-start.17 = (bf16[112,256]{1,0:T(8,128)(2,1)S(1)}, bf16[112,256]{1,0:T(8,128)(2,1)S(1)}, u32[]{:S(2)}, u32[]{:S(2)}) collective-permute-start(bf16[112,256]{1,0:T(8,128)(2,1)S(1)} %add_convert_fusion.7), channel_id=1, source_target_pairs={{0,8},{4,12},{8,0},{12,4},{16,24},{20,28},{24,16},{28,20},{1,9},{5... | collective-permute-start | bytes 172040 | tf_op jit(solution)/shard_map/ppermute | solution.py:609
  83.3 1.5 %collective-permute-start.25 = (bf16[224,256]{1,0:T(8,128)(2,1)S(1)}, bf16[224,256]{1,0:T(8,128)(2,1)S(1)}, u32[]{:S(2)}, u32[]{:S(2)}) collective-permute-start(bf16[224,256]{1,0:T(8,128)(2,1)S(1)} %pad_maximum_fusion.5), channel_id=1, source_target_pairs={{0,4},{4,0},{8,12},{12,8},{16,20},{20,16},{24,28},{28,24},{1,5},{5... | collective-permute-start | bytes 344072 | tf_op jit(solution)/shard_map/ppermute | solution.py:609
  85.4 2.8 %collective-permute-start.18 = (bf16[224,256]{1,0:T(8,128)(2,1)S(1)}, bf16[224,256]{1,0:T(8,128)(2,1)S(1)}, u32[]{:S(2)}, u32[]{:S(2)}) collective-permute-start(bf16[224,256]{1,0:T(8,128)(2,1)S(1)} %pad_maximum_fusion.4), channel_id=1, source_target_pairs={{0,4},{4,0},{8,12},{12,8},{16,20},{20,16},{24,28},{28,24},{1,5},{5... | collective-permute-start | bytes 344072 | tf_op jit(solution)/shard_map/ppermute | solution.py:609
  91.9 2.4 %collective-permute-done.26 = bf16[448,256]{1,0:T(8,128)(2,1)S(1)} collective-permute-done((bf16[448,256]{1,0:T(8,128)(2,1)S(1)}, bf16[448,256]{1,0:T(8,128)(2,1)S(1)}, u32[]{:S(2)}, u32[]{:S(2)}) %collective-permute-start.26) | collective-permute-done | bytes 229408 | tf_op jit(solution)/shard_map/ppermute | solution.py:591
  94.4 2.6 %edge_out.1 = bf16[4096,256]{1,0:T(8,128)(2,1)} custom-call(bf16[4096,256]{1,0:T(8,128)(2,1)S(1)} %get-tuple-element.153.hidden_grad, bf16[1792,256]{1,0:T(8,128)(2,1)S(1)} %copy-done.4), custom_call_target="tpu_custom_call" | custom-call | flops 3300000000 | bytes 1048576 | tf_op jit(solution)/shard_map/edge_out/pallas_call | solution.py:693
  (137 shorter events, 31.4 us)
Async XLA Ops:
  2.8 7.8 %collective-permute-start = (bf16[128,256]{1,0:T(8,128)(2,1)S(1)}, bf16[128,256]{1,0:T(8,128)(2,1)S(1)}, u32[]{:S(2)}, u32[]{:S(2)}) collective-permute-start(bf16[128,256]{1,0:T(8,128)(2,1)S(1)} %get-tuple-element.87), channel_id=1, source_target_pairs={{0,16},{4,20},{8,24},{12,28},{16,0},{20,4},{24,8},{28,12},{1,17},{... | collective-permute-start | bytes 196616 | tf_op jit(solution)/shard_map/ppermute | solution.py:609
  7.4 9.3 %collective-permute-start.1 = (bf16[256,256]{1,0:T(8,128)(2,1)S(1)}, bf16[256,256]{1,0:T(8,128)(2,1)S(1)}, u32[]{:S(2)}, u32[]{:S(2)}) collective-permute-start(bf16[256,256]{1,0:T(8,128)(2,1)S(1)} %get-tuple-element.89), channel_id=1, source_target_pairs={{0,1},{1,0},{2,3},{3,2},{4,5},{5,4},{6,7},{7,6},{8,9},{9,8},{10,11... | collective-permute-start | bytes 393224 | tf_op jit(solution)/shard_map/ppermute | solution.py:587
  10.6 4.4 %collective-permute-start.2 = (bf16[128,256]{1,0:T(8,128)(2,1)S(1)}, bf16[128,256]{1,0:T(8,128)(2,1)S(1)}, u32[]{:S(2)}, u32[]{:S(2)}) collective-permute-start(bf16[128,256]{1,0:T(8,128)(2,1)S(1)} %pad_maximum_fusion.6), channel_id=1, source_target_pairs={{0,8},{4,12},{8,0},{12,4},{16,24},{20,28},{24,16},{28,20},{1,9},{5... | collective-permute-start | bytes 196616 | tf_op jit(solution)/shard_map/ppermute | solution.py:609
  15.0 4.3 %collective-permute-start.3 = (bf16[128,256]{1,0:T(8,128)(2,1)S(1)}, bf16[128,256]{1,0:T(8,128)(2,1)S(1)}, u32[]{:S(2)}, u32[]{:S(2)}) collective-permute-start(bf16[128,256]{1,0:T(8,128)(2,1)S(1)} %pad_maximum_fusion.7), channel_id=1, source_target_pairs={{0,4},{4,0},{8,12},{12,8},{16,20},{20,16},{24,28},{28,24},{1,5},{5... | collective-permute-start | bytes 196616 | tf_op jit(solution)/shard_map/ppermute | solution.py:609
  16.8 8.9 %collective-permute-start.4 = (bf16[256,256]{1,0:T(8,128)(2,1)S(1)}, bf16[256,256]{1,0:T(8,128)(2,1)S(1)}, u32[]{:S(2)}, u32[]{:S(2)}) collective-permute-start(bf16[256,256]{1,0:T(8,128)(2,1)S(1)} %convert_element_type.104), channel_id=1, source_target_pairs={{0,2},{1,3},{2,0},{3,1},{4,6},{5,7},{6,4},{7,5},{8,10},{9,11},{10,... | collective-permute-start | bytes 393224 | tf_op jit(solution)/shard_map/ppermute | solution.py:591
  25.8 8.0 %collective-permute-start.8 = (bf16[256,256]{1,0:T(8,128)(2,1)S(1)}, bf16[256,256]{1,0:T(8,128)(2,1)S(1)}, u32[]{:S(2)}, u32[]{:S(2)}) collective-permute-start(bf16[256,256]{1,0:T(8,128)(2,1)S(1)} %add_convert_fusion.2.cot_mine), channel_id=1, source_target_pairs={{0,1},{1,0},{2,3},{3,2},{4,5},{5,4},{6,7},{7,6},{8,9},{9,8},{10,11... | collective-permute-start | bytes 393224 | tf_op jit(solution)/shard_map/ppermute | solution.py:587
  27.2 6.4 %collective-permute-start.6 = (bf16[256,256]{1,0:T(8,128)(2,1)S(1)}, bf16[256,256]{1,0:T(8,128)(2,1)S(1)}, u32[]{:S(2)}, u32[]{:S(2)}) collective-permute-start(bf16[256,256]{1,0:T(8,128)(2,1)S(1)} %fusion), channel_id=1, source_target_pairs={{0,2},{1,3},{2,0},{3,1},{4,6},{5,7},{6,4},{7,5},{8,10},{9,11},{10,... | collective-permute-start | bytes 393224 | tf_op jit(solution)/shard_map/ppermute | solution.py:591
  54.3 8.2 %collective-permute-start.21 = (bf16[224,256]{1,0:T(8,128)(2,1)S(1)}, bf16[224,256]{1,0:T(8,128)(2,1)S(1)}, u32[]{:S(2)}, u32[]{:S(2)}) collective-permute-start(bf16[224,256]{1,0:T(8,128)(2,1)S(1)} %get-tuple-element.156), channel_id=1, source_target_pairs={{0,4},{4,0},{8,12},{12,8},{16,20},{20,16},{24,28},{28,24},{1,5},{5... | collective-permute-start | bytes 344072 | tf_op jit(solution)/shard_map/ppermute | solution.py:609
  55.8 6.7 %collective-permute-start.10 = (bf16[128,256]{1,0:T(8,128)(2,1)S(1)}, bf16[128,256]{1,0:T(8,128)(2,1)S(1)}, u32[]{:S(2)}, u32[]{:S(2)}) collective-permute-start(bf16[128,256]{1,0:T(8,128)(2,1)S(1)} %get-tuple-element.149), channel_id=1, source_target_pairs={{0,16},{4,20},{8,24},{12,28},{16,0},{20,4},{24,8},{28,12},{1,17},{... | collective-permute-start | bytes 196616 | tf_op jit(solution)/shard_map/ppermute | solution.py:609
  59.0 7.1 %collective-permute-start.11 = (bf16[448,256]{1,0:T(8,128)(2,1)S(1)}, bf16[448,256]{1,0:T(8,128)(2,1)S(1)}, u32[]{:S(2)}, u32[]{:S(2)}) collective-permute-start(bf16[448,256]{1,0:T(8,128)(2,1)S(1)} %slice.92), channel_id=1, source_target_pairs={{0,2},{1,3},{2,0},{3,1},{4,6},{5,7},{6,4},{7,5},{8,10},{9,11},{10,... | collective-permute-start | bytes 688136 | tf_op jit(solution)/shard_map/ppermute | solution.py:609
  66.2 4.2 %collective-permute-start.22 = (bf16[112,256]{1,0:T(8,128)(2,1)S(1)}, bf16[112,256]{1,0:T(8,128)(2,1)S(1)}, u32[]{:S(2)}, u32[]{:S(2)}) collective-permute-start(bf16[112,256]{1,0:T(8,128)(2,1)S(1)} %slice.103), channel_id=1, source_target_pairs={{0,8},{4,12},{8,0},{12,4},{16,24},{20,28},{24,16},{28,20},{1,9},{5... | collective-permute-start | bytes 172040 | tf_op jit(solution)/shard_map/ppermute | solution.py:609
  66.8 4.9 %collective-permute-start.13 = (bf16[224,256]{1,0:T(8,128)(2,1)S(1)}, bf16[224,256]{1,0:T(8,128)(2,1)S(1)}, u32[]{:S(2)}, u32[]{:S(2)}) collective-permute-start(bf16[224,256]{1,0:T(8,128)(2,1)S(1)} %slice.95), channel_id=1, source_target_pairs={{0,4},{4,0},{8,12},{12,8},{16,20},{20,16},{24,28},{28,24},{1,5},{5... | collective-permute-start | bytes 344072 | tf_op jit(solution)/shard_map/ppermute | solution.py:609
  67.3 4.3 %collective-permute-start.12 = (bf16[128,256]{1,0:T(8,128)(2,1)S(1)}, bf16[128,256]{1,0:T(8,128)(2,1)S(1)}, u32[]{:S(2)}, u32[]{:S(2)}) collective-permute-start(bf16[128,256]{1,0:T(8,128)(2,1)S(1)} %pad_maximum_fusion.8), channel_id=1, source_target_pairs={{0,8},{4,12},{8,0},{12,4},{16,24},{20,28},{24,16},{28,20},{1,9},{5... | collective-permute-start | bytes 196616 | tf_op jit(solution)/shard_map/ppermute | solution.py:609
  71.7 4.3 %collective-permute-start.15 = (bf16[112,256]{1,0:T(8,128)(2,1)S(1)}, bf16[112,256]{1,0:T(8,128)(2,1)S(1)}, u32[]{:S(2)}, u32[]{:S(2)}) collective-permute-start(bf16[112,256]{1,0:T(8,128)(2,1)S(1)} %slice.100), channel_id=1, source_target_pairs={{0,8},{4,12},{8,0},{12,4},{16,24},{20,28},{24,16},{28,20},{1,9},{5... | collective-permute-start | bytes 172040 | tf_op jit(solution)/shard_map/ppermute | solution.py:609
  73.2 5.7 %collective-permute-start.23 = (bf16[112,256]{1,0:T(8,128)(2,1)S(1)}, bf16[112,256]{1,0:T(8,128)(2,1)S(1)}, u32[]{:S(2)}, u32[]{:S(2)}) collective-permute-start(bf16[112,256]{1,0:T(8,128)(2,1)S(1)} %add_convert_fusion.6), channel_id=1, source_target_pairs={{0,16},{4,20},{8,24},{12,28},{16,0},{20,4},{24,8},{28,12},{1,17},{... | collective-permute-start | bytes 172040 | tf_op jit(solution)/shard_map/ppermute | solution.py:609
  73.6 15.5 %collective-permute-start.14 = (bf16[128,256]{1,0:T(8,128)(2,1)S(1)}, bf16[128,256]{1,0:T(8,128)(2,1)S(1)}, u32[]{:S(2)}, u32[]{:S(2)}) collective-permute-start(bf16[128,256]{1,0:T(8,128)(2,1)S(1)} %pad_maximum_fusion.9), channel_id=1, source_target_pairs={{0,4},{4,0},{8,12},{12,8},{16,20},{20,16},{24,28},{28,24},{1,5},{5... | collective-permute-start | bytes 196616 | tf_op jit(solution)/shard_map/ppermute | solution.py:609
  76.0 5.1 %collective-permute-start.16 = (bf16[112,256]{1,0:T(8,128)(2,1)S(1)}, bf16[112,256]{1,0:T(8,128)(2,1)S(1)}, u32[]{:S(2)}, u32[]{:S(2)}) collective-permute-start(bf16[112,256]{1,0:T(8,128)(2,1)S(1)} %add_convert_fusion.8), channel_id=1, source_target_pairs={{0,16},{4,20},{8,24},{12,28},{16,0},{20,4},{24,8},{28,12},{1,17},{... | collective-permute-start | bytes 172040 | tf_op jit(solution)/shard_map/ppermute | solution.py:609
  79.0 4.3 %collective-permute-start.24 = (bf16[112,256]{1,0:T(8,128)(2,1)S(1)}, bf16[112,256]{1,0:T(8,128)(2,1)S(1)}, u32[]{:S(2)}, u32[]{:S(2)}) collective-permute-start(bf16[112,256]{1,0:T(8,128)(2,1)S(1)} %add_convert_fusion.5), channel_id=1, source_target_pairs={{0,8},{4,12},{8,0},{12,4},{16,24},{20,28},{24,16},{28,20},{1,9},{5... | collective-permute-start | bytes 172040 | tf_op jit(solution)/shard_map/ppermute | solution.py:609
  81.2 4.2 %collective-permute-start.17 = (bf16[112,256]{1,0:T(8,128)(2,1)S(1)}, bf16[112,256]{1,0:T(8,128)(2,1)S(1)}, u32[]{:S(2)}, u32[]{:S(2)}) collective-permute-start(bf16[112,256]{1,0:T(8,128)(2,1)S(1)} %add_convert_fusion.7), channel_id=1, source_target_pairs={{0,8},{4,12},{8,0},{12,4},{16,24},{20,28},{24,16},{28,20},{1,9},{5... | collective-permute-start | bytes 172040 | tf_op jit(solution)/shard_map/ppermute | solution.py:609
  83.3 4.9 %collective-permute-start.25 = (bf16[224,256]{1,0:T(8,128)(2,1)S(1)}, bf16[224,256]{1,0:T(8,128)(2,1)S(1)}, u32[]{:S(2)}, u32[]{:S(2)}) collective-permute-start(bf16[224,256]{1,0:T(8,128)(2,1)S(1)} %pad_maximum_fusion.5), channel_id=1, source_target_pairs={{0,4},{4,0},{8,12},{12,8},{16,20},{20,16},{24,28},{28,24},{1,5},{5... | collective-permute-start | bytes 344072 | tf_op jit(solution)/shard_map/ppermute | solution.py:609
  85.4 5.5 %collective-permute-start.18 = (bf16[224,256]{1,0:T(8,128)(2,1)S(1)}, bf16[224,256]{1,0:T(8,128)(2,1)S(1)}, u32[]{:S(2)}, u32[]{:S(2)}) collective-permute-start(bf16[224,256]{1,0:T(8,128)(2,1)S(1)} %pad_maximum_fusion.4), channel_id=1, source_target_pairs={{0,4},{4,0},{8,12},{12,8},{16,20},{20,16},{24,28},{28,24},{1,5},{5... | collective-permute-start | bytes 344072 | tf_op jit(solution)/shard_map/ppermute | solution.py:609
  88.2 6.1 %collective-permute-start.26 = (bf16[448,256]{1,0:T(8,128)(2,1)S(1)}, bf16[448,256]{1,0:T(8,128)(2,1)S(1)}, u32[]{:S(2)}, u32[]{:S(2)}) collective-permute-start(bf16[448,256]{1,0:T(8,128)(2,1)S(1)} %pad_maximum_fusion.3), channel_id=1, source_target_pairs={{0,2},{1,3},{2,0},{3,1},{4,6},{5,7},{6,4},{7,5},{8,10},{9,11},{10,... | collective-permute-start | bytes 688136 | tf_op jit(solution)/shard_map/ppermute | solution.py:591
  91.0 6.1 %collective-permute-start.19 = (bf16[448,256]{1,0:T(8,128)(2,1)S(1)}, bf16[448,256]{1,0:T(8,128)(2,1)S(1)}, u32[]{:S(2)}, u32[]{:S(2)}) collective-permute-start(bf16[448,256]{1,0:T(8,128)(2,1)S(1)} %pad_maximum_fusion.2), channel_id=1, source_target_pairs={{0,2},{1,3},{2,0},{3,1},{4,6},{5,7},{6,4},{7,5},{8,10},{9,11},{10,... | collective-permute-start | bytes 688136 | tf_op jit(solution)/shard_map/ppermute | solution.py:609
  94.3 3.3 %collective-permute-start.27 = (bf16[896,256]{1,0:T(8,128)(2,1)S(1)}, bf16[896,256]{1,0:T(8,128)(2,1)S(1)}, u32[]{:S(2)}, u32[]{:S(2)}) collective-permute-start(bf16[896,256]{1,0:T(8,128)(2,1)S(1)} %pad_maximum_fusion.1.mine), channel_id=1, source_target_pairs={{0,1},{1,0},{2,3},{3,2},{4,5},{5,4},{6,7},{7,6},{8,9},{9,8},{10,11... | collective-permute-start | bytes 1376264 | tf_op jit(solution)/shard_map/ppermute | solution.py:587
  (30 other events, 164.0 us)

commit v2 on v1

--- a/solution.py
+++ b/solution.py
@@ -835,8 +835,9 @@
         fine_out_kernel, "fine_out", 2, [per_node],
         [aggregate_rows, coarse_table, after(refined, other)],
     )
-    coarse_received = flip(after(coarse_other, fine_out), "dom", 0)
-    ties = [fine_out]
+    coarse_received = flip(after(coarse_other, other), "dom", 0)
+    ties = [other]
+    received = after(received, fine_out)
     mine, other = halved(add(mine, received))
 
     received = flip(other, "dom", 0)

time: 101 us -> 97.7 us (0.967)
  waiting for transfers between devices: 21.7 us -> 17.2 us
  starting transfers between devices: 33 us -> 34.5 us
    ppermute x20, waiting for transfers between devices: 17.1 us -> 12.6 us  [flip(): return lax.ppermute(value, axis, [(i, i ^ 1 << bit) for i in range(size)])]
    ppermute x20, starting transfers between devices: 28 us -> 29.4 us  [flip(): return lax.ppermute(value, axis, [(i, i ^ 1 << bit) for i in range(size)])]
  transfers between devices with their start and end apart: 28 -> 28, of which waited for: 16 -> 17; matrix products, arithmetic and copies ran while one was open for 0% -> 0% of each run, Pallas kernels for 21% -> 23%
where the time goes in v2:
time: 97.7 us; the launch traced here: 97.5 us
  Pallas kernels  40.2 us (41%)
  starting transfers between devices  34.5 us (35%)
  waiting for transfers between devices  17.2 us (18%)
  local copies, waits for them, and re-layouts  3.21 us (3%)
  between operations  1.79 us (2%)
    pallas_call x16, Pallas kernels, call(): kernel_call(kernel, micros, limit, out_shape=outs, in_specs=in_specs, out...  40.2 us
    ppermute x20, starting transfers between devices, flip(): return lax.ppermute(value, axis, [(i, i ^ 1 << bit) for i in range(size)])  29.4 us
    ppermute x20, waiting for transfers between devices, flip(): return lax.ppermute(value, axis, [(i, i ^ 1 << bit) for i in range(size)])  12.6 us
    ppermute x3, starting transfers between devices, turn_chip(): lax.ppermute(value, 'grp', [(i, (i + 2 * places) % groups) for i in range...  4.28 us
    unnamed x52, local copies, waits for them, and re-layouts  3.14 us
    ppermute x3, waiting for transfers between devices, turn_chip(): lax.ppermute(value, 'grp', [(i, (i + 2 * places) % groups) for i in range...  2.47 us
    ppermute x5, waiting for transfers between devices, swap_core(): return lax.ppermute(value, 'grp', [(i, i ^ 1) for i in range(groups)])  2.17 us
  transfers between devices with their start and end apart: 28, of which 17 were waited for; matrix products, arithmetic and copies ran while one was open for 0% of the time, Pallas kernels for 23%

profile of v2, /device:TPU:0, one launch (start us, length us, event | category | flops | bytes accessed | tf_op | source)
XLA Modules:
  0.0 97.5 jit_solution(4883434876794117346)
XLA Ops:
  2.8 4.1 %collective-permute-start = (bf16[128,256]{1,0:T(8,128)(2,1)S(1)}, bf16[128,256]{1,0:T(8,128)(2,1)S(1)}, u32[]{:S(2)}, u32[]{:S(2)}) collective-permute-start(bf16[128,256]{1,0:T(8,128)(2,1)S(1)} %get-tuple-element.88), channel_id=1, source_target_pairs={{0,16},{4,20},{8,24},{12,28},{16,0},{20,4},{24,8},{28,12},{1,17},{... | collective-permute-start | bytes 196616 | tf_op jit(solution)/shard_map/ppermute | solution.py:609
  11.3 3.7 %fine_local.1.partial = bf16[4096,256]{1,0:T(8,128)(2,1)S(1)} custom-call(bf16[4096,256]{1,0:T(8,128)(2,1)S(1)} %copy-done.2, s32[32,128]{1,0:T(8,128)S(1)} %bitcast.10, bf16[4096,128]{1,0:T(8,128)(2,1)S(1)} %get-tuple-element.87.recv_rows, bf16[1024,256]{1,0:T(8,128)(2,1)S(1)} %copy-done.7, bf16[1792,256]{1,0:T(8,128)(2,1)S(1)} %copy-done.4), custom_call_target="tpu_custom_call" | custom-call | flops 5500000256 | bytes 1048576 | tf_op jit(solution)/shard_map/fine_local/pallas_call | solution.py:693
  15.0 1.7 %collective-permute-start.3 = (bf16[128,256]{1,0:T(8,128)(2,1)S(1)}, bf16[128,256]{1,0:T(8,128)(2,1)S(1)}, u32[]{:S(2)}, u32[]{:S(2)}) collective-permute-start(bf16[128,256]{1,0:T(8,128)(2,1)S(1)} %pad_maximum_fusion.7), channel_id=1, source_target_pairs={{0,4},{4,0},{8,12},{12,8},{16,20},{20,16},{24,28},{28,24},{1,5},{5... | collective-permute-start | bytes 196616 | tf_op jit(solution)/shard_map/ppermute | solution.py:609
  16.8 1.6 %collective-permute-start.4 = (bf16[256,256]{1,0:T(8,128)(2,1)S(1)}, bf16[256,256]{1,0:T(8,128)(2,1)S(1)}, u32[]{:S(2)}, u32[]{:S(2)}) collective-permute-start(bf16[256,256]{1,0:T(8,128)(2,1)S(1)} %convert_element_type.104), channel_id=1, source_target_pairs={{0,2},{1,3},{2,0},{3,1},{4,6},{5,7},{6,4},{7,5},{8,10},{9,11},{10,... | collective-permute-start | bytes 393224 | tf_op jit(solution)/shard_map/ppermute | solution.py:591
  19.3 5.0 %fine_halo.1 = (bf16[4096,256]{1,0:T(8,128)(2,1)S(1)}, bf16[4096,256]{1,0:T(8,128)(2,1)S(1)}, bf16[4096,256]{1,0:T(8,128)(2,1)S(1)}, f32[4096,1]{1,0:T(8,128)S(1...) custom-call(bf16[4096,256]{1,0:T(8,128)(2,1)S(1)} %fine_local.1.part, ...), custom_call_target="tpu_custom_call" | custom-call | flops 6600000000 | bytes 1048576 | tf_op jit(solution)/shard_map/fine_halo/pallas_call | solution.py:693
  27.2 1.7 %collective-permute-start.6 = (bf16[256,256]{1,0:T(8,128)(2,1)S(1)}, bf16[256,256]{1,0:T(8,128)(2,1)S(1)}, u32[]{:S(2)}, u32[]{:S(2)}) collective-permute-start(bf16[256,256]{1,0:T(8,128)(2,1)S(1)} %fusion), channel_id=1, source_target_pairs={{0,2},{1,3},{2,0},{3,1},{4,6},{5,7},{6,4},{7,5},{8,10},{9,11},{10,... | collective-permute-start | bytes 393224 | tf_op jit(solution)/shard_map/ppermute | solution.py:591
  29.0 1.8 %coarse_pre.1 = (bf16[2048,256]{1,0:T(8,128)(2,1)S(1)}, bf16[2048,512]{1,0:T(8,128)(2,1)S(1)}, bf16[512,2048]{1,0:T(8,128)(2,1)S(1)}, bf16[2048,128]{1,0:T(8,128)(2,1)S(1)}, bf16[128,2048]{1,0:T(8,128)(2,1)S(1)}) custom-call(bf16[2048,256]{1,0:T(8,128)(2,1)S(1)} %bitcast.7, s32[16,128]{1,0:T(8,128)S(1)} %bitcast.13, s32[16,128]{1,0:T(8,128)S(1)} %bitcast.14, ...), custom_call_target="tpu_custom_call" | custom-call | flops 2200000000 | bytes 1048576 | tf_op jit(solution)/shard_map/coarse_pre/pallas_call | solution.py:693
  30.8 2.8 %sender_one_hots.1.send_columns = bf16[1280,4096]{1,0:T(8,128)(2,1)S(1)} custom-call(s32[32,128]{1,0:T(8,128)S(1)} %bitcast.11), custom_call_target="tpu_custom_call" | custom-call | flops 1100000000 | bytes 1048576 | tf_op jit(solution)/shard_map/sender_one_hots/pallas_call | solution.py:693
  35.1 6.1 %coarse_both_ways.1 = (bf16[512,256]{1,0:T(8,128)(2,1)S(1)}, bf16[512,256]{1,0:T(8,128)(2,1)S(1)}, bf16[512,256]{1,0:T(8,128)(2,1)S(1)}, bf16[512,256]{1,0:T(8,1...) custom-call(bf16[256,256]{1,0:T(8,128)(2,1)S(1)} %multiply_convert_f, ...), custom_call_target="tpu_custom_call" | custom-call | flops 8800000000 | bytes 1048576 | tf_op jit(solution)/shard_map/coarse_both_ways/pallas_call | solution.py:693
  41.3 2.1 %node_back.1 = (f32[1024,256]{1,0:T(8,128)S(1)}, bf16[1024,256]{1,0:T(8,128)(2,1)S(1)}, bf16[768,256]{1,0:T(8,128)(2,1)S(1)}) custom-call(s32[8,128]{1,0:T(8,128)S(1)} %bitcast.17, bf16[512,256]{1,0:T(8,128)(2,1)S(1)} %get-tuple-element.120.table_grad, bf16[1024,256]{1,0:T(8,128)(2,1)S(1)} %copy-done.5, ...), custom_call_target="tpu_custom_call" | custom-call | flops 5500000256 | bytes 1048576 | tf_op jit(solution)/shard_map/node_back/pallas_call | solution.py:693
  43.4 7.6 %edge_back.1 = (bf16[4096,256]{1,0:T(8,128)(2,1)S(1)}, bf16[1024,256]{1,0:T(8,128)(2,1)S(1)}, bf16[1024,256]{1,0:T(8,128)(2,1)S(1)}, bf16[896,256]{1,0:T(8,128)(...) custom-call(bf16[4096,256]{1,0:T(8,128)(2,1)S(1)} %copy-done.2, ...), custom_call_target="tpu_custom_call" | custom-call | flops 8800000000 | bytes 1048576 | tf_op jit(solution)/shard_map/edge_back/pallas_call | solution.py:693
  53.9 3.2 %collective-permute-start.10 = (bf16[128,256]{1,0:T(8,128)(2,1)S(1)}, bf16[128,256]{1,0:T(8,128)(2,1)S(1)}, u32[]{:S(2)}, u32[]{:S(2)}) collective-permute-start(bf16[128,256]{1,0:T(8,128)(2,1)S(1)} %get-tuple-element.150), channel_id=1, source_target_pairs={{0,16},{4,20},{8,24},{12,28},{16,0},{20,4},{24,8},{28,12},{1,17},{... | collective-permute-start | bytes 196616 | tf_op jit(solution)/shard_map/ppermute | solution.py:609
  57.1 1.5 %collective-permute-start.21 = (bf16[224,256]{1,0:T(8,128)(2,1)S(1)}, bf16[224,256]{1,0:T(8,128)(2,1)S(1)}, u32[]{:S(2)}, u32[]{:S(2)}) collective-permute-start(bf16[224,256]{1,0:T(8,128)(2,1)S(1)} %get-tuple-element.158), channel_id=1, source_target_pairs={{0,4},{4,0},{8,12},{12,8},{16,20},{20,16},{24,28},{28,24},{1,5},{5... | collective-permute-start | bytes 344072 | tf_op jit(solution)/shard_map/ppermute | solution.py:609
  62.7 1.5 %collective-permute-start.13 = (bf16[224,256]{1,0:T(8,128)(2,1)S(1)}, bf16[224,256]{1,0:T(8,128)(2,1)S(1)}, u32[]{:S(2)}, u32[]{:S(2)}) collective-permute-start(bf16[224,256]{1,0:T(8,128)(2,1)S(1)} %slice.95), channel_id=1, source_target_pairs={{0,4},{4,0},{8,12},{12,8},{16,20},{20,16},{24,28},{28,24},{1,5},{5... | collective-permute-start | bytes 344072 | tf_op jit(solution)/shard_map/ppermute | solution.py:609
  64.2 1.5 %collective-permute-start.12 = (bf16[128,256]{1,0:T(8,128)(2,1)S(1)}, bf16[128,256]{1,0:T(8,128)(2,1)S(1)}, u32[]{:S(2)}, u32[]{:S(2)}) collective-permute-start(bf16[128,256]{1,0:T(8,128)(2,1)S(1)} %pad_maximum_fusion.8), channel_id=1, source_target_pairs={{0,8},{4,12},{8,0},{12,4},{16,24},{20,28},{24,16},{28,20},{1,9},{5... | collective-permute-start | bytes 196616 | tf_op jit(solution)/shard_map/ppermute | solution.py:609
  66.6 1.9 %collective-permute-done.12.refs_2_ = bf16[128,256]{1,0:T(8,128)(2,1)S(1)} collective-permute-done((bf16[128,256]{1,0:T(8,128)(2,1)S(1)}, bf16[128,256]{1,0:T(8,128)(2,1)S(1)}, u32[]{:S(2)}, u32[]{:S(2)}) %collective-permute-start.12) | collective-permute-done | bytes 65568 | tf_op jit(solution)/shard_map/ppermute | solution.py:609
  68.5 1.6 %collective-permute-start.15 = (bf16[112,256]{1,0:T(8,128)(2,1)S(1)}, bf16[112,256]{1,0:T(8,128)(2,1)S(1)}, u32[]{:S(2)}, u32[]{:S(2)}) collective-permute-start(bf16[112,256]{1,0:T(8,128)(2,1)S(1)} %slice.100), channel_id=1, source_target_pairs={{0,8},{4,12},{8,0},{12,4},{16,24},{20,28},{24,16},{28,20},{1,9},{5... | collective-permute-start | bytes 172040 | tf_op jit(solution)/shard_map/ppermute | solution.py:609
  70.1 2.0 %collective-permute-start.23 = (bf16[112,256]{1,0:T(8,128)(2,1)S(1)}, bf16[112,256]{1,0:T(8,128)(2,1)S(1)}, u32[]{:S(2)}, u32[]{:S(2)}) collective-permute-start(bf16[112,256]{1,0:T(8,128)(2,1)S(1)} %add_convert_fusion.6), channel_id=1, source_target_pairs={{0,16},{4,20},{8,24},{12,28},{16,0},{20,4},{24,8},{28,12},{1,17},{... | collective-permute-start | bytes 172040 | tf_op jit(solution)/shard_map/ppermute | solution.py:609
  72.8 2.6 %collective-permute-start.16 = (bf16[112,256]{1,0:T(8,128)(2,1)S(1)}, bf16[112,256]{1,0:T(8,128)(2,1)S(1)}, u32[]{:S(2)}, u32[]{:S(2)}) collective-permute-start(bf16[112,256]{1,0:T(8,128)(2,1)S(1)} %add_convert_fusion.8), channel_id=1, source_target_pairs={{0,16},{4,20},{8,24},{12,28},{16,0},{20,4},{24,8},{28,12},{1,17},{... | collective-permute-start | bytes 172040 | tf_op jit(solution)/shard_map/ppermute | solution.py:609
  76.4 1.5 %collective-permute-done.16 = bf16[112,256]{1,0:T(8,128)(2,1)S(1)} collective-permute-done((bf16[112,256]{1,0:T(8,128)(2,1)S(1)}, bf16[112,256]{1,0:T(8,128)(2,1)S(1)}, u32[]{:S(2)}, u32[]{:S(2)}) %collective-permute-start.16) | collective-permute-done | bytes 57376 | tf_op jit(solution)/shard_map/ppermute | solution.py:609
  77.9 2.1 %collective-permute-start.17 = (bf16[112,256]{1,0:T(8,128)(2,1)S(1)}, bf16[112,256]{1,0:T(8,128)(2,1)S(1)}, u32[]{:S(2)}, u32[]{:S(2)}) collective-permute-start(bf16[112,256]{1,0:T(8,128)(2,1)S(1)} %add_convert_fusion.7), channel_id=1, source_target_pairs={{0,8},{4,12},{8,0},{12,4},{16,24},{20,28},{24,16},{28,20},{1,9},{5... | collective-permute-start | bytes 172040 | tf_op jit(solution)/shard_map/ppermute | solution.py:609
  82.2 2.0 %collective-permute-start.18 = (bf16[224,256]{1,0:T(8,128)(2,1)S(1)}, bf16[224,256]{1,0:T(8,128)(2,1)S(1)}, u32[]{:S(2)}, u32[]{:S(2)}) collective-permute-start(bf16[224,256]{1,0:T(8,128)(2,1)S(1)} %pad_maximum_fusion.4), channel_id=1, source_target_pairs={{0,4},{4,0},{8,12},{12,8},{16,20},{20,16},{24,28},{28,24},{1,5},{5... | collective-permute-start | bytes 344072 | tf_op jit(solution)/shard_map/ppermute | solution.py:609
  88.9 2.5 %collective-permute-done.26 = bf16[448,256]{1,0:T(8,128)(2,1)S(1)} collective-permute-done((bf16[448,256]{1,0:T(8,128)(2,1)S(1)}, bf16[448,256]{1,0:T(8,128)(2,1)S(1)}, u32[]{:S(2)}, u32[]{:S(2)}) %collective-permute-start.26) | collective-permute-done | bytes 229408 | tf_op jit(solution)/shard_map/ppermute | solution.py:591
  91.5 2.6 %edge_out.1 = bf16[4096,256]{1,0:T(8,128)(2,1)} custom-call(bf16[4096,256]{1,0:T(8,128)(2,1)S(1)} %get-tuple-element.155.hidden_grad, bf16[1792,256]{1,0:T(8,128)(2,1)S(1)} %copy-done.4), custom_call_target="tpu_custom_call" | custom-call | flops 3300000000 | bytes 1048576 | tf_op jit(solution)/shard_map/edge_out/pallas_call | solution.py:693
  (137 shorter events, 31.1 us)
Async XLA Ops:
  2.8 7.8 %collective-permute-start = (bf16[128,256]{1,0:T(8,128)(2,1)S(1)}, bf16[128,256]{1,0:T(8,128)(2,1)S(1)}, u32[]{:S(2)}, u32[]{:S(2)}) collective-permute-start(bf16[128,256]{1,0:T(8,128)(2,1)S(1)} %get-tuple-element.88), channel_id=1, source_target_pairs={{0,16},{4,20},{8,24},{12,28},{16,0},{20,4},{24,8},{28,12},{1,17},{... | collective-permute-start | bytes 196616 | tf_op jit(solution)/shard_map/ppermute | solution.py:609
  7.4 9.3 %collective-permute-start.1 = (bf16[256,256]{1,0:T(8,128)(2,1)S(1)}, bf16[256,256]{1,0:T(8,128)(2,1)S(1)}, u32[]{:S(2)}, u32[]{:S(2)}) collective-permute-start(bf16[256,256]{1,0:T(8,128)(2,1)S(1)} %get-tuple-element.90), channel_id=1, source_target_pairs={{0,1},{1,0},{2,3},{3,2},{4,5},{5,4},{6,7},{7,6},{8,9},{9,8},{10,11... | collective-permute-start | bytes 393224 | tf_op jit(solution)/shard_map/ppermute | solution.py:587
  10.6 4.4 %collective-permute-start.2 = (bf16[128,256]{1,0:T(8,128)(2,1)S(1)}, bf16[128,256]{1,0:T(8,128)(2,1)S(1)}, u32[]{:S(2)}, u32[]{:S(2)}) collective-permute-start(bf16[128,256]{1,0:T(8,128)(2,1)S(1)} %pad_maximum_fusion.6), channel_id=1, source_target_pairs={{0,8},{4,12},{8,0},{12,4},{16,24},{20,28},{24,16},{28,20},{1,9},{5... | collective-permute-start | bytes 196616 | tf_op jit(solution)/shard_map/ppermute | solution.py:609
  15.0 4.3 %collective-permute-start.3 = (bf16[128,256]{1,0:T(8,128)(2,1)S(1)}, bf16[128,256]{1,0:T(8,128)(2,1)S(1)}, u32[]{:S(2)}, u32[]{:S(2)}) collective-permute-start(bf16[128,256]{1,0:T(8,128)(2,1)S(1)} %pad_maximum_fusion.7), channel_id=1, source_target_pairs={{0,4},{4,0},{8,12},{12,8},{16,20},{20,16},{24,28},{28,24},{1,5},{5... | collective-permute-start | bytes 196616 | tf_op jit(solution)/shard_map/ppermute | solution.py:609
  16.8 8.9 %collective-permute-start.4 = (bf16[256,256]{1,0:T(8,128)(2,1)S(1)}, bf16[256,256]{1,0:T(8,128)(2,1)S(1)}, u32[]{:S(2)}, u32[]{:S(2)}) collective-permute-start(bf16[256,256]{1,0:T(8,128)(2,1)S(1)} %convert_element_type.104), channel_id=1, source_target_pairs={{0,2},{1,3},{2,0},{3,1},{4,6},{5,7},{6,4},{7,5},{8,10},{9,11},{10,... | collective-permute-start | bytes 393224 | tf_op jit(solution)/shard_map/ppermute | solution.py:591
  25.8 8.0 %collective-permute-start.8 = (bf16[256,256]{1,0:T(8,128)(2,1)S(1)}, bf16[256,256]{1,0:T(8,128)(2,1)S(1)}, u32[]{:S(2)}, u32[]{:S(2)}) collective-permute-start(bf16[256,256]{1,0:T(8,128)(2,1)S(1)} %add_convert_fusion.2.cot_mine), channel_id=1, source_target_pairs={{0,1},{1,0},{2,3},{3,2},{4,5},{5,4},{6,7},{7,6},{8,9},{9,8},{10,11... | collective-permute-start | bytes 393224 | tf_op jit(solution)/shard_map/ppermute | solution.py:587
  27.2 6.4 %collective-permute-start.6 = (bf16[256,256]{1,0:T(8,128)(2,1)S(1)}, bf16[256,256]{1,0:T(8,128)(2,1)S(1)}, u32[]{:S(2)}, u32[]{:S(2)}) collective-permute-start(bf16[256,256]{1,0:T(8,128)(2,1)S(1)} %fusion), channel_id=1, source_target_pairs={{0,2},{1,3},{2,0},{3,1},{4,6},{5,7},{6,4},{7,5},{8,10},{9,11},{10,... | collective-permute-start | bytes 393224 | tf_op jit(solution)/shard_map/ppermute | solution.py:591
  53.0 9.0 %collective-permute-start.11 = (bf16[448,256]{1,0:T(8,128)(2,1)S(1)}, bf16[448,256]{1,0:T(8,128)(2,1)S(1)}, u32[]{:S(2)}, u32[]{:S(2)}) collective-permute-start(bf16[448,256]{1,0:T(8,128)(2,1)S(1)} %slice.92), channel_id=1, source_target_pairs={{0,2},{1,3},{2,0},{3,1},{4,6},{5,7},{6,4},{7,5},{8,10},{9,11},{10,... | collective-permute-start | bytes 688136 | tf_op jit(solution)/shard_map/ppermute | solution.py:609
  53.9 6.7 %collective-permute-start.10 = (bf16[128,256]{1,0:T(8,128)(2,1)S(1)}, bf16[128,256]{1,0:T(8,128)(2,1)S(1)}, u32[]{:S(2)}, u32[]{:S(2)}) collective-permute-start(bf16[128,256]{1,0:T(8,128)(2,1)S(1)} %get-tuple-element.150), channel_id=1, source_target_pairs={{0,16},{4,20},{8,24},{12,28},{16,0},{20,4},{24,8},{28,12},{1,17},{... | collective-permute-start | bytes 196616 | tf_op jit(solution)/shard_map/ppermute | solution.py:609
  57.1 4.8 %collective-permute-start.21 = (bf16[224,256]{1,0:T(8,128)(2,1)S(1)}, bf16[224,256]{1,0:T(8,128)(2,1)S(1)}, u32[]{:S(2)}, u32[]{:S(2)}) collective-permute-start(bf16[224,256]{1,0:T(8,128)(2,1)S(1)} %get-tuple-element.158), channel_id=1, source_target_pairs={{0,4},{4,0},{8,12},{12,8},{16,20},{20,16},{24,28},{28,24},{1,5},{5... | collective-permute-start | bytes 344072 | tf_op jit(solution)/shard_map/ppermute | solution.py:609
  62.1 4.5 %collective-permute-start.22 = (bf16[112,256]{1,0:T(8,128)(2,1)S(1)}, bf16[112,256]{1,0:T(8,128)(2,1)S(1)}, u32[]{:S(2)}, u32[]{:S(2)}) collective-permute-start(bf16[112,256]{1,0:T(8,128)(2,1)S(1)} %slice.103), channel_id=1, source_target_pairs={{0,8},{4,12},{8,0},{12,4},{16,24},{20,28},{24,16},{28,20},{1,9},{5... | collective-permute-start | bytes 172040 | tf_op jit(solution)/shard_map/ppermute | solution.py:609
  62.7 5.8 %collective-permute-start.13 = (bf16[224,256]{1,0:T(8,128)(2,1)S(1)}, bf16[224,256]{1,0:T(8,128)(2,1)S(1)}, u32[]{:S(2)}, u32[]{:S(2)}) collective-permute-start(bf16[224,256]{1,0:T(8,128)(2,1)S(1)} %slice.95), channel_id=1, source_target_pairs={{0,4},{4,0},{8,12},{12,8},{16,20},{20,16},{24,28},{28,24},{1,5},{5... | collective-permute-start | bytes 344072 | tf_op jit(solution)/shard_map/ppermute | solution.py:609
  64.2 4.3 %collective-permute-start.12 = (bf16[128,256]{1,0:T(8,128)(2,1)S(1)}, bf16[128,256]{1,0:T(8,128)(2,1)S(1)}, u32[]{:S(2)}, u32[]{:S(2)}) collective-permute-start(bf16[128,256]{1,0:T(8,128)(2,1)S(1)} %pad_maximum_fusion.8), channel_id=1, source_target_pairs={{0,8},{4,12},{8,0},{12,4},{16,24},{20,28},{24,16},{28,20},{1,9},{5... | collective-permute-start | bytes 196616 | tf_op jit(solution)/shard_map/ppermute | solution.py:609
  68.5 4.2 %collective-permute-start.15 = (bf16[112,256]{1,0:T(8,128)(2,1)S(1)}, bf16[112,256]{1,0:T(8,128)(2,1)S(1)}, u32[]{:S(2)}, u32[]{:S(2)}) collective-permute-start(bf16[112,256]{1,0:T(8,128)(2,1)S(1)} %slice.100), channel_id=1, source_target_pairs={{0,8},{4,12},{8,0},{12,4},{16,24},{20,28},{24,16},{28,20},{1,9},{5... | collective-permute-start | bytes 172040 | tf_op jit(solution)/shard_map/ppermute | solution.py:609
  70.1 6.0 %collective-permute-start.23 = (bf16[112,256]{1,0:T(8,128)(2,1)S(1)}, bf16[112,256]{1,0:T(8,128)(2,1)S(1)}, u32[]{:S(2)}, u32[]{:S(2)}) collective-permute-start(bf16[112,256]{1,0:T(8,128)(2,1)S(1)} %add_convert_fusion.6), channel_id=1, source_target_pairs={{0,16},{4,20},{8,24},{12,28},{16,0},{20,4},{24,8},{28,12},{1,17},{... | collective-permute-start | bytes 172040 | tf_op jit(solution)/shard_map/ppermute | solution.py:609
  72.0 14.2 %collective-permute-start.14 = (bf16[128,256]{1,0:T(8,128)(2,1)S(1)}, bf16[128,256]{1,0:T(8,128)(2,1)S(1)}, u32[]{:S(2)}, u32[]{:S(2)}) collective-permute-start(bf16[128,256]{1,0:T(8,128)(2,1)S(1)} %pad_maximum_fusion.9), channel_id=1, source_target_pairs={{0,4},{4,0},{8,12},{12,8},{16,20},{20,16},{24,28},{28,24},{1,5},{5... | collective-permute-start | bytes 196616 | tf_op jit(solution)/shard_map/ppermute | solution.py:609
  72.8 5.1 %collective-permute-start.16 = (bf16[112,256]{1,0:T(8,128)(2,1)S(1)}, bf16[112,256]{1,0:T(8,128)(2,1)S(1)}, u32[]{:S(2)}, u32[]{:S(2)}) collective-permute-start(bf16[112,256]{1,0:T(8,128)(2,1)S(1)} %add_convert_fusion.8), channel_id=1, source_target_pairs={{0,16},{4,20},{8,24},{12,28},{16,0},{20,4},{24,8},{28,12},{1,17},{... | collective-permute-start | bytes 172040 | tf_op jit(solution)/shard_map/ppermute | solution.py:609
  76.1 4.2 %collective-permute-start.24 = (bf16[112,256]{1,0:T(8,128)(2,1)S(1)}, bf16[112,256]{1,0:T(8,128)(2,1)S(1)}, u32[]{:S(2)}, u32[]{:S(2)}) collective-permute-start(bf16[112,256]{1,0:T(8,128)(2,1)S(1)} %add_convert_fusion.5), channel_id=1, source_target_pairs={{0,8},{4,12},{8,0},{12,4},{16,24},{20,28},{24,16},{28,20},{1,9},{5... | collective-permute-start | bytes 172040 | tf_op jit(solution)/shard_map/ppermute | solution.py:609
  77.9 4.2 %collective-permute-start.17 = (bf16[112,256]{1,0:T(8,128)(2,1)S(1)}, bf16[112,256]{1,0:T(8,128)(2,1)S(1)}, u32[]{:S(2)}, u32[]{:S(2)}) collective-permute-start(bf16[112,256]{1,0:T(8,128)(2,1)S(1)} %add_convert_fusion.7), channel_id=1, source_target_pairs={{0,8},{4,12},{8,0},{12,4},{16,24},{20,28},{24,16},{28,20},{1,9},{5... | collective-permute-start | bytes 172040 | tf_op jit(solution)/shard_map/ppermute | solution.py:609
  80.4 4.9 %collective-permute-start.25 = (bf16[224,256]{1,0:T(8,128)(2,1)S(1)}, bf16[224,256]{1,0:T(8,128)(2,1)S(1)}, u32[]{:S(2)}, u32[]{:S(2)}) collective-permute-start(bf16[224,256]{1,0:T(8,128)(2,1)S(1)} %pad_maximum_fusion.5), channel_id=1, source_target_pairs={{0,4},{4,0},{8,12},{12,8},{16,20},{20,16},{24,28},{28,24},{1,5},{5... | collective-permute-start | bytes 344072 | tf_op jit(solution)/shard_map/ppermute | solution.py:609
  82.2 5.5 %collective-permute-start.18 = (bf16[224,256]{1,0:T(8,128)(2,1)S(1)}, bf16[224,256]{1,0:T(8,128)(2,1)S(1)}, u32[]{:S(2)}, u32[]{:S(2)}) collective-permute-start(bf16[224,256]{1,0:T(8,128)(2,1)S(1)} %pad_maximum_fusion.4), channel_id=1, source_target_pairs={{0,4},{4,0},{8,12},{12,8},{16,20},{20,16},{24,28},{28,24},{1,5},{5... | collective-permute-start | bytes 344072 | tf_op jit(solution)/shard_map/ppermute | solution.py:609
  85.3 6.1 %collective-permute-start.26 = (bf16[448,256]{1,0:T(8,128)(2,1)S(1)}, bf16[448,256]{1,0:T(8,128)(2,1)S(1)}, u32[]{:S(2)}, u32[]{:S(2)}) collective-permute-start(bf16[448,256]{1,0:T(8,128)(2,1)S(1)} %pad_maximum_fusion.3), channel_id=1, source_target_pairs={{0,2},{1,3},{2,0},{3,1},{4,6},{5,7},{6,4},{7,5},{8,10},{9,11},{10,... | collective-permute-start | bytes 688136 | tf_op jit(solution)/shard_map/ppermute | solution.py:591
  87.7 6.4 %collective-permute-start.19 = (bf16[448,256]{1,0:T(8,128)(2,1)S(1)}, bf16[448,256]{1,0:T(8,128)(2,1)S(1)}, u32[]{:S(2)}, u32[]{:S(2)}) collective-permute-start(bf16[448,256]{1,0:T(8,128)(2,1)S(1)} %pad_maximum_fusion.2), channel_id=1, source_target_pairs={{0,2},{1,3},{2,0},{3,1},{4,6},{5,7},{6,4},{7,5},{8,10},{9,11},{10,... | collective-permute-start | bytes 688136 | tf_op jit(solution)/shard_map/ppermute | solution.py:609
  91.4 3.3 %collective-permute-start.27 = (bf16[896,256]{1,0:T(8,128)(2,1)S(1)}, bf16[896,256]{1,0:T(8,128)(2,1)S(1)}, u32[]{:S(2)}, u32[]{:S(2)}) collective-permute-start(bf16[896,256]{1,0:T(8,128)(2,1)S(1)} %pad_maximum_fusion.1.mine), channel_id=1, source_target_pairs={{0,1},{1,0},{2,3},{3,2},{4,5},{5,4},{6,7},{7,6},{8,9},{9,8},{10,11... | collective-permute-start | bytes 1376264 | tf_op jit(solution)/shard_map/ppermute | solution.py:587
  (30 other events, 161.1 us)
